TPU v7x, 32 devices: a whole 2x2x4 slice. The times are simulated.
32 devices in a mesh: req: 8 (over y, x, core), head: 4 (over z).
Axes of the slice: x: 2, y: 2, z: 4, core: 2. Of those that a mesh axis runs over, the one named last changes fastest.
Arguments:
- hidden: bfloat16 [256, 16, 2048], P('req', None, 'head'), may hold values from -6 to 6
- w_zx: bfloat16 [2048, 2, 4096], P(None, None, 'head'), may hold values from -0.125 to 0.125
- w_bc: bfloat16 [2048, 256], replicated, may hold values from -0.125 to 0.125
- w_dt: bfloat16 [2048, 64], P(None, 'head'), may hold values from -0.125 to 0.125
- conv_x_w: float32 [5, 4096], P(None, 'head'), may hold values from -3 to 3
- conv_bc_w: float32 [5, 256], replicated, may hold values from -3 to 3
- dt_bias: float32 [64], P('head'), may hold values from -4 to 0.5
- a_log: float32 [64], P('head'), may hold values from 0 to 2.5
- d_skip: float32 [64], P('head'), may hold values from 0.5 to 1.5
- norm_gain: float32 [4096], P('head'), may hold values from 0.1 to 1.9
- w_out: bfloat16 [4096, 2048], P('head'), may hold values from -0.09375 to 0.09375
- ssm_state: float32 [256, 64, 64, 128], P('req', 'head'), may hold values from -3 to 3
- conv_x_state: float32 [256, 3, 4096], P('req', None, 'head'), may hold values from -6 to 6
- conv_bc_state: float32 [256, 3, 256], P('req'), may hold values from -6 to 6
- slot: int32 [256], replicated, may hold values from 0 to 255, as said below
- lengths: int32 [256], replicated, may hold values from 0 to 16
- accepted: int32 [256], replicated, may hold values from 0 to 16
Outputs:
- out: bfloat16 [256, 16, 2048], P('req', None, 'head')
- new_state: float32 [256, 64, 64, 128], P('req', 'head')
- new_conv_x: float32 [256, 3, 4096], P('req', None, 'head')
- new_conv_bc: float32 [256, 3, 256], P('req')
Inputs may be any that keep to these rules, and one draw needn't show every extreme that they name: slot is a permutation of the pool rows; the requests of each aligned block of 32 requests have exactly 4 pool rows in each aligned block of 32 pool rows.
All inputs are finite; a program needn't handle non-finite values.
Results may differ from a plain program's by a relative error of at most 0.0082.
Values may be sent and summed in bfloat16 or wider, within the bound.
A program may use at most 128 MiB of HBM per device.

v0:
```python
import jax
import jax.numpy as jnp
from jax import lax
from jax.sharding import PartitionSpec as P

highest = lax.Precision.HIGHEST


def conv_step(previous, inputs, taps):
    window = jnp.concatenate([previous, inputs.astype(jnp.float32)], axis=1)
    tail = taps.shape[0] - 1
    steps = inputs.shape[1]
    total = taps[tail] + taps[0] * window[:, 0:steps]
    for tap in range(1, tail):
        total = total + taps[tap] * window[:, tap : tap + steps]
    return (jax.nn.silu(total).astype(jnp.bfloat16), window)


def keep_rows(window, counted, tail):
    picks = counted[:, None] + jnp.arange(tail, dtype=jnp.int32)[None, :]
    return jnp.take_along_axis(window, picks[:, :, None], axis=1)


def scan_block(x_conv, bc_conv, dt_in, states, counted, dt_bias, a_log, d_skip):
    heads = states.shape[1]
    nstate = states.shape[3]
    blocks, steps, chans = x_conv.shape
    headdim = chans // heads
    xh = x_conv.astype(jnp.float32).reshape(blocks, steps, heads, headdim)
    bmat = bc_conv[..., :nstate].astype(jnp.float32)
    cmat = bc_conv[..., nstate:].astype(jnp.float32)
    step_size = jax.nn.softplus(dt_in.astype(jnp.float32) + dt_bias)
    rate = step_size * -jnp.exp(a_log)
    cumul = jnp.cumsum(rate, axis=1)
    carried = jnp.exp(cumul)[..., None] * jnp.einsum(
        "bhpn,btn->bthp", states, cmat, precision=highest
    )
    inner = jnp.einsum("btn,bsn->bts", cmat, bmat, precision=highest)
    places = jnp.arange(steps, dtype=jnp.int32)
    lower = (places[:, None] >= places[None, :])[None, :, :, None]
    spread = cumul[:, :, None, :] - cumul[:, None, :, :]
    factor = jnp.where(lower, jnp.exp(jnp.where(lower, spread, 0.0)), 0.0)
    factor = factor * inner[..., None] * step_size[:, None, :, :]
    within = jnp.einsum("btsh,bshp->bthp", factor, xh, precision=highest)
    mixed = (
        (carried + within + d_skip[:, None] * xh).reshape(blocks, steps, chans).astype(jnp.bfloat16)
    )
    live = (places[None, :] < counted[:, None])[..., None]
    total = jnp.sum(jnp.where(live, rate, 0.0), axis=1)
    remain = jnp.where(live, total[:, None, :] - cumul, 0.0)
    scaled = jnp.where(live, jnp.exp(remain) * step_size, 0.0)
    updated = jnp.exp(total)[:, :, None, None] * states
    updated = updated + jnp.einsum("bsh,bshp,bsn->bhpn", scaled, xh, bmat, precision=highest)
    return (mixed, updated)


def advance(
    x_pre,
    bc_pre,
    dt_pre,
    conv_x_prev,
    conv_bc_prev,
    states,
    counted,
    conv_x_w,
    conv_bc_w,
    dt_bias,
    a_log,
    d_skip,
):
    tail = conv_x_prev.shape[1]
    x_conv, x_window = conv_step(conv_x_prev, x_pre, conv_x_w)
    bc_conv, bc_window = conv_step(conv_bc_prev, bc_pre, conv_bc_w)
    mixed, updated = scan_block(x_conv, bc_conv, dt_pre, states, counted, dt_bias, a_log, d_skip)
    return (mixed, updated, keep_rows(x_window, counted, tail), keep_rows(bc_window, counted, tail))


def per_device(
    hidden,
    w_zx,
    w_bc,
    w_dt,
    conv_x_w,
    conv_bc_w,
    dt_bias,
    a_log,
    d_skip,
    norm_gain,
    w_out,
    ssm_state,
    conv_x_state,
    conv_bc_state,
    slot,
    lengths,
    accepted,
):
    local_requests, steps, width_part = hidden.shape
    width = w_zx.shape[0]
    local_inner = w_zx.shape[2]
    bc_cols = w_bc.shape[1]
    stacked = jnp.concatenate([w_zx.reshape(width, 2 * local_inner), w_bc, w_dt], axis=1)
    piece = lax.all_gather(hidden, "head", axis=2, tiled=True)
    projected = jnp.dot(
        piece.reshape(-1, piece.shape[2]), stacked, preferred_element_type=jnp.float32
    )
    projected = projected.astype(jnp.bfloat16).reshape(local_requests, steps, -1)
    gate_in = projected[..., :local_inner]
    x_in = projected[..., local_inner : 2 * local_inner]
    bc_in = projected[..., 2 * local_inner : 2 * local_inner + bc_cols]
    dt_in = projected[..., 2 * local_inner + bc_cols :]
    myself = lax.axis_index("req")
    peers = lax.axis_size("req")
    per_peer = local_requests // peers
    slot_blocks = slot.reshape(peers, local_requests)
    owner_blocks = slot_blocks // local_requests
    local_rows = slot_blocks % local_requests
    by_owner = jnp.argsort(owner_blocks, axis=1, stable=True)
    my_order = lax.dynamic_index_in_dim(by_owner, myself, 0, keepdims=False)
    undo_order = jnp.argsort(my_order)
    selected = lax.dynamic_slice_in_dim(by_owner, myself * per_peer, per_peer, 1)
    arrive_rows = jnp.take_along_axis(local_rows, selected, axis=1).reshape(local_requests)
    to_pool = jnp.argsort(arrive_rows)
    counted = jnp.minimum(accepted, lengths)
    counted_blocks = counted.reshape(peers, local_requests)
    my_lengths = lax.dynamic_index_in_dim(
        lengths.reshape(peers, local_requests), myself, 0, keepdims=False
    )
    outgoing = (
        jnp.take(ssm_state, arrive_rows, axis=0),
        jnp.take(conv_x_state, arrive_rows, axis=0),
        jnp.take(conv_bc_state, arrive_rows, axis=0),
    )
    states_in, conv_x_in, conv_bc_in = (
        lax.all_to_all(outgoing[0], "req", split_axis=0, concat_axis=0, tiled=True),
        lax.all_to_all(outgoing[1], "req", split_axis=0, concat_axis=0, tiled=True),
        lax.all_to_all(outgoing[2], "req", split_axis=0, concat_axis=0, tiled=True),
    )
    my_counted = jnp.take(
        lax.dynamic_index_in_dim(counted_blocks, myself, 0, keepdims=False), my_order, axis=0
    )
    mixed_sorted, states_out, conv_x_out, conv_bc_out = advance(
        jnp.take(x_in, my_order, axis=0),
        jnp.take(bc_in, my_order, axis=0),
        jnp.take(dt_in, my_order, axis=0),
        conv_x_in,
        conv_bc_in,
        states_in,
        my_counted,
        conv_x_w,
        conv_bc_w,
        dt_bias,
        a_log,
        d_skip,
    )
    mixed = jnp.take(mixed_sorted, undo_order, axis=0)
    back_states, back_conv_x, back_conv_bc = (
        lax.all_to_all(states_out, "req", split_axis=0, concat_axis=0, tiled=True),
        lax.all_to_all(conv_x_out, "req", split_axis=0, concat_axis=0, tiled=True),
        lax.all_to_all(conv_bc_out, "req", split_axis=0, concat_axis=0, tiled=True),
    )
    new_state = jnp.take(back_states, to_pool, axis=0)
    new_conv_x = jnp.take(back_conv_x, to_pool, axis=0)
    new_conv_bc = jnp.take(back_conv_bc, to_pool, axis=0)
    gated = mixed.astype(jnp.float32) * jax.nn.silu(gate_in.astype(jnp.float32))
    squares = lax.psum(jnp.sum(gated * gated, axis=-1), "head")
    meansq = squares / (local_inner * lax.axis_size("head"))
    normed = (gated * lax.rsqrt(meansq + 1e-05)[..., None] * norm_gain).astype(jnp.bfloat16)
    partial_out = jnp.dot(
        normed.reshape(-1, local_inner), w_out, preferred_element_type=jnp.float32
    ).reshape(local_requests, steps, width)
    summed = lax.psum_scatter(partial_out, "head", scatter_dimension=2, tiled=True)
    places = jnp.arange(steps, dtype=jnp.int32)
    valid = places[None, :] < my_lengths[:, None]
    out = jnp.where(valid[..., None], summed, 0.0).astype(jnp.bfloat16)
    return (out, new_state, new_conv_x, new_conv_bc)


def solution(mesh):
    in_specs = (
        P("req", None, "head"),
        P(None, None, "head"),
        P(),
        P(None, "head"),
        P(None, "head"),
        P(),
        P("head"),
        P("head"),
        P("head"),
        P("head"),
        P("head", None),
        P("req", "head", None, None),
        P("req", None, "head"),
        P("req", None, None),
        P(),
        P(),
        P(),
    )
    out_specs = (
        P("req", None, "head"),
        P("req", "head", None, None),
        P("req", None, "head"),
        P("req", None, None),
    )
    return jax.shard_map(
        per_device, mesh=mesh, in_specs=in_specs, out_specs=out_specs, check_vma=False
    )
```

profile of v0, /device:TPU:0, one launch (start us, length us, event | category | flops | bytes accessed | tf_op | source)
XLA Modules:
  0.0 544.4 jit_solution(5363107016275087201)
XLA Ops:
  7.2 0.7 all-gather.2.cloned.1.call-update
  7.9 0.7 min.3
  8.7 0.8 reshape.276
  9.6 0.8 sort.48
  10.5 0.7 gather_fusion.3
  11.8 1.6 sort.49
  13.4 0.7 gather_fusion.2
  14.7 0.7 gather_fusion.6
  15.9 0.8 copy_select_fusion
  16.7 5.2 all-to-all-start
  22.1 1.1 gather_fusion.8
  23.4 1.1 copy.83
  24.7 10.2 %copy.97 = bf16[256,8,2,1024]{3,1,2,0:T(8,128)(2,1)} copy(bf16[256,8,2,1024]{3,2,1,0:T(2,128)(2,1)} %bitcast.56) | data formatting | bytes 16777216
  34.9 14.7 %gather_fusion.7 = f32[32,16,64,128]{3,2,1,0:T(8,128)} fusion(f32[32,16,64,128]{3,2,1,0:T(8,128)} %param.36, s32[1024]{0:T(1024)S(1)} %pad_clamp_fusion.3), kind=kCustom, calls=%fused_computation.1.clone | custom fusion | bytes 33554560 | tf_op jit(solution)/shard_map/jit(_take)/gather | solution.py:129
  49.7 8.6 %all-gather.2.cloned.1.call-done = bf16[32,16,2048]{2,1,0:T(8,128)(2,1)} async-done(((bf16[32,16,512]{2,1,0:T(8,128)(2,1)}), bf16[32,16,2048]{2,1,0:T(8,128)(2,1)}) %all-gather.2.cloned.1.call-update) | async-done | bytes 2097168 | tf_op jit(solution)/shard_map/all_gather | solution.py:102
  58.3 10.8 %fusion.20 = bf16[512,2320]{0,1:T(8,128)(2,1)} fusion(bf16[512,2048]{1,0:T(8,128)(2,1)} %bitcast.68, bf16[2048,16]{1,0:T(8,128)(2,1)S(1)} %copy.75, bf16[2048,256]{1,0:T(8,128)(2,1)S(1)} %copy-done.35, bf16[2048,2048]{1,0:T(8,128)(2,1)} %bitcast.57), kind=kOutput, calls=%fused_computation.45 | convolution fusion | flops 4895088640 | bytes 13975552 | tf_op jit(solution)/shard_map/dot_general | solution.py:103
  69.1 3.1 copy.76
  72.2 1.5 gather_fusion.1
  73.7 1.1 select_convert_fusion.2
  74.8 4.4 all-to-all-start.2
  79.3 1.0 copy.92
  80.3 2.1 gather_fusion.5
  82.5 0.8 broadcast_select_fusion.6
  83.2 5.7 %all-to-all-done.2 = f32[32,3,1024]{2,1,0:T(4,128)} async-done(((f32[32,3,1024]{2,1,0:T(4,128)}), f32[32,3,1024]{2,1,0:T(4,128)}, u32[]{:S(2)}, u32[]{:S(2)}) %all-to-all-start.2) | async-done | bytes 393248 | tf_op jit(solution)/shard_map/all_to_all | solution.py:135
  88.9 3.4 all-to-all-start.5
  92.3 12.5 %broadcast_select_fusion.1 = f32[32,16,64,128]{3,2,1,0:T(8,128)} fusion(f32[32,16,64,128]{3,2,1,0:T(8,128)} %gather_fusion.7, pred[32]{0:T(512)(128)(4,1)S(1)} %copy-done.17), kind=kLoop, calls=%fused_computation.22 | loop fusion | flops 4194304 | bytes 33554464 | tf_op jit(solution)/shard_map/jit(_take)/select_n | solution.py:129
  105.5 5.7 %all-to-all-start.1 = ((f32[32,16,64,128]{3,2,1,0:T(8,128)}), f32[32,16,64,128]{3,2,1,0:T(8,128)}, u32[]{:S(2)}, u32[]{:S(2)}) async-start(f32[32,16,64,128]{3,2,1,0:T(8,128)} %broadcast_select_fusion.1), calls=%async_computation.1 | async-start | bytes 33554432 | tf_op jit(solution)/shard_map/all_to_all | solution.py:134
  113.2 1.1 slice.125
  114.3 0.7 gather_fusion
  115.3 2.1 multiply_select_fusion
  117.6 2.9 gather_fusion.9
  120.6 1.4 select_convert_fusion
  122.0 1.7 pad_maximum_fusion
  123.7 2.9 copy.91
  126.6 2.4 gather_fusion.4
  129.0 1.0 reshape.381
  130.0 3.8 multiply_convert_fusion.1
  133.8 2.9 reshape.281
  137.3 2.0 broadcast_select_fusion.3
  139.3 155.9 %all-to-all-done.1 = f32[32,16,64,128]{3,2,1,0:T(8,128)} async-done(((f32[32,16,64,128]{3,2,1,0:T(8,128)}), f32[32,16,64,128]{3,2,1,0:T(8,128)}, u32[]{:S(2)}, u32[]{:S(2)}) %all-to-all-start.1) | async-done | bytes 16777248 | tf_op jit(solution)/shard_map/all_to_all | solution.py:134
  295.2 3.9 all-to-all-start.4
  299.1 21.5 %multiply_add_fusion = f32[32,16,64,128]{3,2,1,0:T(8,128)} fusion(f32[32,16,64,128]{3,2,1,0:T(8,128)} %all-to-all-done.1, f32[32,16]{1,0:T(8,128)S(1)} %exp.49, f32[32,16,16]{1,2,0:T(8,128)S(1)} %copy.90, bf16[32,16,16,64]{3,2,1,0:T(8,128)(2,1)S(1)} %reshape.281, bf16[32,16,256]{2,1,0:T(8,128)(2,1)S(1)} %multiply_convert_fusion.3), kind=kOutput, calls=%fused_computation.14 | convolution fusion | flops 814743552 | bytes 36061184 | tf_op jit(solution)/shard_map/bsh,bshp,bsn->bhpn/dot_general | solution.py:53
  320.6 5.7 %all-to-all-start.3 = ((f32[32,16,64,128]{3,2,1,0:T(8,128)}), f32[32,16,64,128]{3,2,1,0:T(8,128)}, u32[]{:S(2)}, u32[]{:S(2)}) async-start(f32[32,16,64,128]{3,2,1,0:T(8,128)} %multiply_add_fusion), calls=%async_computation.4 | async-start | bytes 33554432 | tf_op jit(solution)/shard_map/all_to_all | solution.py:157
  326.4 1.1 copy.78
  327.6 1.8 copy.86
  329.4 1.8 copy.84
  331.4 4.9 fusion.13
  336.3 23.3 %fusion.10 = bf16[32,16,16,64]{3,1,2,0:T(8,128)(2,1)S(1)} fusion(f32[32,16,64,16]{2,3,1,0:T(8,128)S(1)} %fusion.13, f32[32,16,64,128]{3,2,1,0:T(8,128)} %all-to-all-done.1, f32[16]{0:T(128)S(1)} %copy-done.32, f32[32,16,16]{1,2,0:T(8,128)S(1)} %copy.78, bf16[32,16,16,64]{3,2,1,0:T(8,128)(2,1)S(1)} %reshape.281, ...), kind=kOutput, calls=%fused_computation.31 | convolution fusion | flops 808452096 | bytes 24510976 | tf_op jit(solution)/shard_map/bhpn,btn->bthp/dot_general | solution.py:35
  359.6 1.9 copy.89
  361.5 4.2 convert_element_type.54
  365.8 2.8 gather_fusion.10
  368.6 2.1 multiply_reduce_fusion
  370.7 16.9 %psum.7 = f32[32,16]{1,0:T(8,128)S(1)} all-reduce(f32[32,16]{1,0:T(8,128)S(1)} %multiply_reduce_fusion), channel_id=1, replica_groups=mesh['req'=8,'head'=4] {'head'}, use_global_device_ids=true, to_apply=%region_4.9 | all-reduce | flops 512 | bytes 4096 | tf_op jit(solution)/shard_map/psum | solution.py:165
  387.6 7.4 %fusion.11 = f32[32,16,2048]{2,1,0:T(8,128)} fusion(bf16[1024,2048]{1,0:T(8,128)(2,1)} %param.35, f32[1024]{0:T(1024)S(1)} %copy-done.36, f32[32,16]{1,0:T(8,128)S(1)} %add_rsqrt_fusion, bf16[32,16,2320]{2,1,0:T(8,128)(2,1)S(1)} %bitcast.55, bf16[32,16,1024]{2,1,0:T(8,128)(2,1)} %gather_fusion.10, pred[32]{0:T(512)(128)(4,1)S(1)} %copy-done.30), kind=kOutput, calls=%fused_computation.32 | convolution fusion | flops 2153250816 | bytes 10506752 | tf_op jit(solution)/shard_map/dot_general | solution.py:168
  395.0 0.6 copy-done.22
  395.7 1.6 sort.50
  398.2 0.7 copy.94
  398.8 0.9 gather_fusion.12
  399.9 1.0 copy.93
  400.8 69.6 %reduce-scatter.2.cloned.1.call-done = f32[32,16,512]{2,1,0:T(8,128)} async-done(((f32[32,16,2048]{2,1,0:T(8,128)}), f32[32,16,512]{2,1,0:T(8,128)}) %reduce-scatter.2.cloned.1.call-update) | async-done | bytes 1048592 | tf_op jit(solution)/shard_map/reduce_scatter | solution.py:171
  470.5 2.2 select_convert_fusion.1
  472.6 37.7 %all-to-all-done.3 = f32[32,16,64,128]{3,2,1,0:T(8,128)} async-done(((f32[32,16,64,128]{3,2,1,0:T(8,128)}), f32[32,16,64,128]{3,2,1,0:T(8,128)}, u32[]{:S(2)}, u32[]{:S(2)}) %all-to-all-start.3) | async-done | bytes 16777248 | tf_op jit(solution)/shard_map/all_to_all | solution.py:157
  510.3 14.5 %gather_fusion.11 = f32[32,16,64,128]{3,2,1,0:T(8,128)} fusion(f32[32,16,64,128]{3,2,1,0:T(8,128)} %all-to-all-done.3, s32[1024]{0:T(1024)S(1)} %pad_clamp_fusion), kind=kCustom, calls=%fused_computation.5.clone | custom fusion | bytes 33554560 | tf_op jit(solution)/shard_map/jit(_take)/gather | solution.py:161
  524.8 12.5 %broadcast_select_fusion = f32[32,16,64,128]{3,2,1,0:T(8,128)} fusion(f32[32,16,64,128]{3,2,1,0:T(8,128)} %gather_fusion.11, pred[32]{0:T(512)(128)(4,1)S(1)} %compare_and_fusion), kind=kLoop, calls=%fused_computation.21 | loop fusion | flops 4194304 | bytes 33554464 | tf_op jit(solution)/shard_map/jit(_take)/select_n | solution.py:161
  (134 shorter events, 7.7 us)
Async XLA Ops:
  7.2 14.9 %copy-start = (f32[32,3,1024]{2,0,1:T(8,128)S(1)}, f32[32,3,1024]{2,0,1:T(8,128)}, u32[]{:S(2)}) copy-start(f32[32,3,1024]{2,0,1:T(8,128)} %param.37) | copy-start | bytes 1179652
  7.2 7.5 %copy-start.2 = (f32[32,3,256]{2,0,1:T(8,128)S(1)}, f32[32,3,256]{2,0,1:T(8,128)}, u32[]{:S(2)}) copy-start(f32[32,3,256]{2,0,1:T(8,128)} %param.38) | copy-start | bytes 294916
  7.2 51.1 %all-gather.2.cloned.1.call-start = ((), (), s32[]{:S(2)}) async-start(), calls=%async_computation.7 | async-start | bytes 2621440 | tf_op jit(solution)/shard_map/all_gather | solution.py:102
  11.6 10.4 %copy-start.20 = (s32[32]{0:T(128)}, s32[32]{0:T(128)S(1)}, u32[]{:S(2)}) copy-start(s32[32]{0:T(128)S(1)} %select_n.165) | copy-start | bytes 388
  13.4 8.6 %copy-start.33 = (s32[32]{0:T(128)}, s32[32]{0:T(128)S(1)}, u32[]{:S(2)}) copy-start(s32[32]{0:T(128)S(1)} %get-tuple-element.12) | copy-start | bytes 388
  13.4 58.8 %copy-start.18 = (s32[1024]{0:T(1024)}, s32[1024]{0:T(1024)S(1)}, u32[]{:S(2)}) copy-start(s32[1024]{0:T(1024)S(1)} %pad_clamp_fusion.4) | copy-start | bytes 12292
  14.6 35.0 %copy-start.14 = (s32[32]{0:T(128)}, s32[32]{0:T(128)S(1)}, u32[]{:S(2)}) copy-start(s32[32]{0:T(128)S(1)} %get-tuple-element.26) | copy-start | bytes 388
  15.9 8.5 %copy-start.16 = (pred[32]{0:T(512)(128)(4,1)}, pred[32]{0:T(512)(128)(4,1)S(1)}, u32[]{:S(2)}) copy-start(pred[32]{0:T(512)(128)(4,1)S(1)} %get-tuple-element.47) | copy-start | bytes 100
  16.7 58.1 %all-to-all-start = ((f32[32,3,256]{2,1,0:T(4,128)}), f32[32,3,256]{2,1,0:T(4,128)S(1)}, u32[]{:S(2)}, u32[]{:S(2)}) async-start(f32[32,3,256]{2,1,0:T(4,128)} %copy_select_fusion), calls=%async_computation | async-start | bytes 262144 | tf_op jit(solution)/shard_map/all_to_all | solution.py:136
  22.1 2.3 copy-start.7
  34.9 23.4 %copy-start.35 = (bf16[2048,256]{1,0:T(8,128)(2,1)S(1)}, bf16[2048,256]{1,0:T(8,128)(2,1)}, u32[]{:S(2)}) copy-start(bf16[2048,256]{1,0:T(8,128)(2,1)} %param.27) | copy-start | bytes 3145732
  72.2 41.0 %copy-start.3 = (bf16[512,2320]{1,0:T(8,128)(2,1)}, bf16[512,2320]{1,0:T(8,128)(2,1)S(1)}, u32[]{:S(2)}) copy-start(bf16[512,2320]{1,0:T(8,128)(2,1)S(1)} %copy.76) | copy-start | bytes 7127044
  74.8 17.5 %copy-start.17 = (pred[32]{0:T(512)(128)(4,1)S(1)}, pred[32]{0:T(512)(128)(4,1)}, u32[]{:S(2)}) copy-start(pred[32]{0:T(512)(128)(4,1)} %copy-done.16) | copy-start | bytes 100
  74.8 14.1 %all-to-all-start.2 = ((f32[32,3,1024]{2,1,0:T(4,128)}), f32[32,3,1024]{2,1,0:T(4,128)}, u32[]{:S(2)}, u32[]{:S(2)}) async-start(f32[32,3,1024]{2,1,0:T(4,128)} %copy.83), calls=%async_computation.2 | async-start | bytes 1048576 | tf_op jit(solution)/shard_map/all_to_all | solution.py:135
  88.9 15.9 %all-to-all-start.5 = ((f32[32,3,256]{2,1,0:T(4,128)}), f32[32,3,256]{2,1,0:T(4,128)S(1)}, u32[]{:S(2)}, u32[]{:S(2)}) async-start(f32[32,3,256]{2,1,0:T(4,128)} %broadcast_select_fusion.6), calls=%async_computation.6 | async-start | bytes 262144 | tf_op jit(solution)/shard_map/all_to_all | solution.py:159
  104.8 6.5 %copy-start.31 = (s32[32]{0:T(128)S(1)}, s32[32]{0:T(128)}, u32[]{:S(2)}) copy-start(s32[32]{0:T(128)} %get-tuple-element.43) | copy-start | bytes 388
  104.8 7.1 %copy-start.37 = (f32[16]{0:T(128)S(1)}, f32[16]{0:T(128)}, u32[]{:S(2)}) copy-start(f32[16]{0:T(128)} %param.32) | copy-start | bytes 196
  104.8 7.1 %copy-start.15 = (s32[32]{0:T(128)S(1)}, s32[32]{0:T(128)}, u32[]{:S(2)}) copy-start(s32[32]{0:T(128)} %copy-done.14) | copy-start | bytes 388
  104.8 7.1 %copy-start.28 = (f32[5,256]{1,0:T(8,128)S(1)}, f32[5,256]{1,0:T(8,128)}, u32[]{:S(2)}) copy-start(f32[5,256]{1,0:T(8,128)} %param.30) | copy-start | bytes 15364
  104.8 7.7 %copy-start.13 = (f32[5,1024]{1,0:T(8,128)S(1)}, f32[5,1024]{1,0:T(8,128)}, u32[]{:S(2)}) copy-start(f32[5,1024]{1,0:T(8,128)} %param.29) | copy-start | bytes 61444
  104.8 10.2 %copy-start.19 = (f32[16]{0:T(128)S(1)}, f32[16]{0:T(128)}, u32[]{:S(2)}) copy-start(f32[16]{0:T(128)} %param.31) | copy-start | bytes 196
  104.8 0.7 copy-start.5
  105.5 189.7 %all-to-all-start.1 = ((f32[32,16,64,128]{3,2,1,0:T(8,128)}), f32[32,16,64,128]{3,2,1,0:T(8,128)}, u32[]{:S(2)}, u32[]{:S(2)}) async-start(f32[32,16,64,128]{3,2,1,0:T(8,128)} %broadcast_select_fusion.1), calls=%async_computation.1 | async-start | bytes 33554432 | tf_op jit(solution)/shard_map/all_to_all | solution.py:134
  111.9 3.5 copy-start.29
  126.6 3.4 copy-start.8
  126.6 3.4 copy-start.9
  126.6 3.4 copy-start.10
  126.6 3.4 copy-start.11
  126.6 3.4 copy-start.12
  130.0 6.8 %copy-start.23 = (f32[1,256]{1,0:T(1,128)S(1)}, f32[1,256]{1,0:T(1,128)}, u32[]{:S(2)}) copy-start(f32[1,256]{1,0:T(1,128)} %get-tuple-element.36) | copy-start | bytes 3076
  130.0 6.8 %copy-start.24 = (f32[1,256]{1,0:T(1,128)S(1)}, f32[1,256]{1,0:T(1,128)}, u32[]{:S(2)}) copy-start(f32[1,256]{1,0:T(1,128)} %get-tuple-element.37) | copy-start | bytes 3076
  130.0 6.8 %copy-start.25 = (f32[1,256]{1,0:T(1,128)S(1)}, f32[1,256]{1,0:T(1,128)}, u32[]{:S(2)}) copy-start(f32[1,256]{1,0:T(1,128)} %get-tuple-element.38) | copy-start | bytes 3076
  130.0 6.8 %copy-start.26 = (f32[1,256]{1,0:T(1,128)S(1)}, f32[1,256]{1,0:T(1,128)}, u32[]{:S(2)}) copy-start(f32[1,256]{1,0:T(1,128)} %get-tuple-element.39) | copy-start | bytes 3076
  130.0 6.8 %copy-start.27 = (f32[1,256]{1,0:T(1,128)S(1)}, f32[1,256]{1,0:T(1,128)}, u32[]{:S(2)}) copy-start(f32[1,256]{1,0:T(1,128)} %get-tuple-element.40) | copy-start | bytes 3076
  295.2 25.4 %all-to-all-start.4 = ((f32[32,3,1024]{2,1,0:T(4,128)}), f32[32,3,1024]{2,1,0:T(4,128)S(1)}, u32[]{:S(2)}, u32[]{:S(2)}) async-start(f32[32,3,1024]{2,1,0:T(4,128)} %broadcast_select_fusion.3), calls=%async_computation.5 | async-start | bytes 1048576 | tf_op jit(solution)/shard_map/all_to_all | solution.py:158
  320.6 5.8 %copy-start.34 = (s32[32]{0:T(128)S(1)}, s32[32]{0:T(128)}, u32[]{:S(2)}) copy-start(s32[32]{0:T(128)} %copy-done.33) | copy-start | bytes 388
  320.6 189.7 %all-to-all-start.3 = ((f32[32,16,64,128]{3,2,1,0:T(8,128)}), f32[32,16,64,128]{3,2,1,0:T(8,128)}, u32[]{:S(2)}, u32[]{:S(2)}) async-start(f32[32,16,64,128]{3,2,1,0:T(8,128)} %multiply_add_fusion), calls=%async_computation.4 | async-start | bytes 33554432 | tf_op jit(solution)/shard_map/all_to_all | solution.py:157
  326.3 144.1 %reduce-scatter.2.cloned.1.call-start = ((), (), s32[]{:S(2)}) async-start(), calls=%async_computation.8 | async-start | bytes 5242880 | tf_op jit(solution)/shard_map/reduce_scatter | solution.py:171
  331.4 4.9 copy-start.32
  361.5 7.1 %copy-start.4 = (bf16[512,2320]{1,0:T(8,128)(2,1)S(1)}, bf16[512,2320]{1,0:T(8,128)(2,1)}, u32[]{:S(2)}) copy-start(bf16[512,2320]{1,0:T(8,128)(2,1)} %copy-done.3) | copy-start | bytes 7127044
  361.5 7.1 %copy-start.30 = (pred[32]{0:T(512)(128)(4,1)S(1)}, pred[32]{0:T(512)(128)(4,1)}, u32[]{:S(2)}) copy-start(pred[32]{0:T(512)(128)(4,1)} %get-tuple-element.46) | copy-start | bytes 100
  361.5 26.0 %copy-start.36 = (f32[1024]{0:T(1024)S(1)}, f32[1024]{0:T(1024)}, u32[]{:S(2)}) copy-start(f32[1024]{0:T(1024)} %param.34) | copy-start | bytes 12292
  394.9 0.7 copy-start.22
  394.9 0.8 copy-start.21
  394.9 2.5 copy-start.6
  524.8 12.5 %copy-start.1 = (f32[32,3,1024]{2,0,1:T(8,128)S(1)}, f32[32,3,1024]{2,0,1:T(8,128)}, u32[]{:S(2)}) copy-start(f32[32,3,1024]{2,0,1:T(8,128)} %param.37) | copy-start | bytes 1179652
Sparse Core Ops, SparseCore 0:
  9.6 48.6 all-gather.1
  395.1 75.3 reduce-scatter.1
where the time goes:
time: 554 us; the launch traced here: 544 us
  waiting for transfers between devices  278 us (50%)
  local copies, waits for them, and re-layouts  87.3 us (16%)
  matrix products  68 us (12%)
  other arithmetic  50.7 us (9%)
  starting transfers between devices  28.4 us (5%)
  blocking collectives  16.9 us (3%)
  between operations  14.9 us (3%)
    all_to_all x1, waiting for transfers between devices, per_device(): lax.all_to_all(outgoing[0], 'req', split_axis=0, concat_axis=0, tiled=True)  156 us
    reduce_scatter x1, waiting for transfers between devices, per_device(): lax.psum_scatter(partial_out, 'head', scatter_dimension=2, tiled=True)  69.6 us
    all_to_all x1, waiting for transfers between devices, per_device(): lax.all_to_all(states_out, 'req', split_axis=0, concat_axis=0, tiled=True)  37.7 us
    dot_general x1, matrix products, scan_block(): jnp.einsum('bhpn,btn->bthp', states, cmat, precision=highest)  23.3 us
    dot_general x1, matrix products, scan_block(): jnp.einsum('bsh,bshp,bsn->bhpn', scaled, xh, bmat, precision=highest)  21.5 us
    psum x1, blocking collectives, per_device(): squares = lax.psum(jnp.sum(gated * gated, axis=-1), 'head')  16.9 us
    gather x1, local copies, waits for them, and re-layouts, per_device(): jnp.take(ssm_state, arrive_rows, axis=0)  14.7 us
    gather x1, local copies, waits for them, and re-layouts, per_device(): new_state = jnp.take(back_states, to_pool, axis=0)  14.5 us
  transfers between devices with their start and end apart: 8, of which 5 were waited for; matrix products, arithmetic and copies ran while one was open for 33% of the time, Pallas kernels for 0%

commit v1 on v0

v1 whole, which is shorter than its diff:
```python
import functools

import jax
import jax.numpy as jnp
from jax import lax
from jax.experimental import pallas as pl
from jax.experimental.pallas import tpu as pltpu
from jax.sharding import PartitionSpec as P

highest = lax.Precision.HIGHEST
f32 = jnp.float32
bf16 = jnp.bfloat16


def iota(shape, dim):
    return lax.broadcasted_iota(jnp.int32, shape, dim)


def dot_nt(a, b):
    return lax.dot_general(a, b, (((1,), (1,)), ((), ())), preferred_element_type=f32)


def dot_nn(a, b, precision=None):
    return jnp.dot(a, b, preferred_element_type=f32, precision=precision)


def silu(v):
    return v * (1.0 / (1.0 + jnp.exp(-v)))


def conv(window_ref, prev_ref, inputs, taps, keep_ref, count_of, group, steps, tail):
    base = 8 - tail
    chans = inputs.shape[-1]
    window_ref[:, 0:8, :] = jnp.zeros((group, 8, inputs.shape[-1]), f32)
    window_ref[:, base:8, :] = prev_ref[...]
    window_ref[:, 8 : 8 + steps, :] = inputs.reshape(group, steps, chans)
    total = taps[tail + 1 : tail + 2, :][None]
    for tap in range(tail + 1):
        total = total + taps[tap : tap + 1, :][None] * window_ref[:, base + tap : base + tap + steps, :]
    for r in range(group):
        held = window_ref[r, :, :]
        place = iota((8 + steps, 1), 0) - base - count_of(r)
        for k in range(tail):
            keep_ref[r, k : k + 1, :] = jnp.sum(jnp.where(place == k, held, 0.0), axis=0, keepdims=True)
    return silu(total).astype(bf16).reshape(group * steps, chans)


def core_kernel(
    group,
    counted_ref,
    zx_ref,
    bcdt_ref,
    state_ref,
    cx_ref,
    cbc_ref,
    cxw_ref,
    cbw_ref,
    heads_ref,
    gain_ref,
    g_ref,
    sq_ref,
    new_state_ref,
    ncx_ref,
    ncbc_ref,
    xwin,
    bcwin,
):
    heads, headdim, nstate = state_ref.shape[1:]
    chans = heads * headdim
    tokens = zx_ref.shape[0]
    steps = tokens // group
    tail = cx_ref.shape[1]
    first = pl.program_id(0) * group

    def count_of(r):
        return counted_ref[first + r]

    bcdt = bcdt_ref[...].astype(f32)
    x = conv(xwin, cx_ref, zx_ref[:, chans:].astype(f32), cxw_ref[...], ncx_ref, count_of, group, steps, tail)
    bc = conv(bcwin, cbc_ref, bcdt[:, : 2 * nstate], cbw_ref[...], ncbc_ref, count_of, group, steps, tail)
    bmat, cmat = bc[:, :nstate], bc[:, nstate:]
    xf = x.astype(f32)

    dt_bias, a_log, d_skip = heads_ref[0:1, :], heads_ref[1:2, :], heads_ref[2:3, :]
    raw = bcdt[:, 2 * nstate :] + dt_bias
    dt = jnp.maximum(raw, 0.0) + jnp.log1p(jnp.exp(-jnp.abs(raw)))
    rate = dt * -jnp.exp(a_log)

    row, col = iota((tokens, tokens), 0), iota((tokens, tokens), 1)
    same = row // steps == col // steps
    lower = jnp.where(same & (row >= col), 1.0, 0.0)
    cumul = dot_nn(lower, rate, highest)
    token = iota((tokens, heads), 0)
    limit = jnp.zeros((tokens, heads), jnp.int32)
    for r in range(group):
        limit = jnp.where(token // steps == r, count_of(r), limit)
    live = (token % steps) < limit
    total = dot_nn(jnp.where(same, 1.0, 0.0), jnp.where(live, rate, 0.0), highest)
    scaled = jnp.where(live, jnp.exp(jnp.where(live, total - cumul, 0.0)) * dt, 0.0)
    spread_to = jnp.where(iota((heads, chans), 1) // headdim == iota((heads, chans), 0), 1.0, 0.0).astype(bf16)
    dt_e = dot_nn(dt.astype(bf16), spread_to)
    scaled_e = dot_nn(scaled.astype(bf16), spread_to)
    carry_e = dot_nn(jnp.exp(cumul).astype(bf16), spread_to)
    skip_hi = d_skip.astype(bf16)
    skip_lo = (d_skip - skip_hi.astype(f32)).astype(bf16)
    skip_e = dot_nn(jnp.broadcast_to(skip_hi, (8, heads)), spread_to) + dot_nn(
        jnp.broadcast_to(skip_lo, (8, heads)), spread_to
    )
    mixed_skip = skip_e[0:1, :] * xf
    dtx = (dt_e * xf).astype(bf16)
    sxt = (scaled_e * xf).T.astype(bf16)
    btok = iota((tokens, nstate), 0) // steps
    bsel = jnp.concatenate([jnp.where(btok == r, bmat.astype(f32), 0.0) for r in range(group)], axis=1).astype(bf16)
    grown = dot_nn(sxt, bsel)

    wide = heads * steps
    spread_hs = jnp.where(iota((heads, wide), 1) // steps == iota((heads, wide), 0), 1.0, 0.0)
    cumul_hs = dot_nn(cumul, spread_hs, highest)
    t_at, s_at = iota((steps, wide), 0), iota((steps, wide), 1) % steps
    block = (iota((wide, chans), 0) // steps == iota((wide, chans), 1) // headdim).astype(f32).astype(bf16)
    eye = iota((heads, heads), 0) == iota((heads, heads), 1)

    pieces = []
    for r in range(group):
        span = slice(r * steps, (r + 1) * steps)
        c_r = cmat[span, :]
        b_r = bmat[span, :]
        inner = dot_nt(c_r, jnp.concatenate([b_r] * heads, axis=0))
        here = cumul_hs[span, :]
        there = jnp.sum(jnp.where(t_at == s_at, here, 0.0), axis=0, keepdims=True)
        factor = jnp.where(t_at >= s_at, jnp.exp(jnp.where(t_at >= s_at, here - there, 0.0)) * inner, 0.0)
        spreaded = jnp.concatenate([dtx[span, :]] * heads, axis=0) * block
        within = dot_nn(factor.astype(bf16), spreaded)
        states = state_ref[r].reshape(chans, nstate)
        carried = dot_nt(c_r, states.astype(bf16))
        pieces.append(carry_e[span, :] * carried + within)
        decay = jnp.sum(jnp.where(eye, jnp.exp(total[r * steps : r * steps + 1, :]), 0.0), axis=1, keepdims=True)
        for h in range(heads):
            new_state_ref[r, h] = (
                state_ref[r, h] * decay[h : h + 1, :]
                + grown[h * headdim : (h + 1) * headdim, r * nstate : (r + 1) * nstate]
            )
    mixed = (jnp.concatenate(pieces, axis=0) + mixed_skip).astype(bf16).astype(f32)
    gated = mixed * silu(zx_ref[:, :chans].astype(f32))
    sq_ref[...] = jnp.sum(gated * gated, axis=1, keepdims=True)
    g_ref[...] = (gated * gain_ref[...]).astype(bf16)


def core(counted, zx, bcdt, states, cx, cbc, cxw, cbw, head_params, gain, group):
    rows, heads, headdim, nstate = states.shape
    chans = heads * headdim
    steps = zx.shape[0] // rows
    tail = cx.shape[1]
    tokens = group * steps

    def step_block(*shape):
        return pl.BlockSpec(shape, lambda i, c: (i,) + (0,) * (len(shape) - 1))

    def whole(a):
        return pl.BlockSpec(a.shape, lambda i, c: (0,) * a.ndim)

    return pl.pallas_call(
        functools.partial(core_kernel, group),
        grid_spec=pltpu.PrefetchScalarGridSpec(
            num_scalar_prefetch=1,
            grid=(rows // group,),
            in_specs=[
                step_block(tokens, 2 * chans),
                step_block(tokens, bcdt.shape[1]),
                step_block(group, heads, headdim, nstate),
                step_block(group, tail, chans),
                step_block(group, tail, 2 * nstate),
                whole(cxw),
                whole(cbw),
                whole(head_params),
                whole(gain),
            ],
            out_specs=[
                step_block(tokens, chans),
                step_block(tokens, 1),
                step_block(group, heads, headdim, nstate),
                step_block(group, tail, chans),
                step_block(group, tail, 2 * nstate),
            ],
            scratch_shapes=[
                pltpu.VMEM((group, 8 + steps, chans), f32),
                pltpu.VMEM((group, 8 + steps, 2 * nstate), f32),
            ],
        ),
        out_shape=[
            jax.ShapeDtypeStruct((rows * steps, chans), bf16),
            jax.ShapeDtypeStruct((rows * steps, 1), f32),
            jax.ShapeDtypeStruct(states.shape, f32),
            jax.ShapeDtypeStruct(cx.shape, f32),
            jax.ShapeDtypeStruct(cbc.shape, f32),
        ],
        compiler_params=pltpu.CompilerParams(vmem_limit_bytes=48 * 1024 * 1024),
        name="core",
    )(counted, zx, bcdt, states, cx, cbc, cxw, cbw, head_params, gain)


def routes(slot, rows, myself, peers):
    per_peer = rows // peers
    blocks = slot.reshape(peers, rows)
    owner = blocks // rows
    earlier = jnp.arange(rows)[None, :, None] > jnp.arange(rows)[None, None, :]
    rank = jnp.sum((owner[:, :, None] == owner[:, None, :]) & earlier, axis=2, dtype=jnp.int32)
    places = jnp.arange(rows, dtype=jnp.int32)
    my_owner = lax.dynamic_index_in_dim(owner, myself, 0, keepdims=False)
    my_rank = lax.dynamic_index_in_dim(rank, myself, 0, keepdims=False)
    home = my_owner * per_peer + my_rank
    send_order = jnp.sum(jnp.where(home[None, :] == places[:, None], places[None, :], 0), axis=1, dtype=jnp.int32)
    arrive = (jnp.arange(peers, dtype=jnp.int32)[:, None] * per_peer + rank).reshape(-1)
    flat = slot.reshape(-1)
    hit = flat[None, :] == (myself * rows + places)[:, None]
    to_pool = jnp.sum(jnp.where(hit, arrive[None, :], 0), axis=1, dtype=jnp.int32)
    request = jnp.sum(jnp.where(hit, jnp.arange(flat.shape[0], dtype=jnp.int32)[None, :], 0), axis=1, dtype=jnp.int32)
    back_order = jnp.sum(jnp.where(to_pool[None, :] == places[:, None], places[None, :], 0), axis=1, dtype=jnp.int32)
    return send_order, to_pool, back_order, home, request


def per_device(
    hidden,
    w_zx,
    w_bc,
    w_dt,
    conv_x_w,
    conv_bc_w,
    dt_bias,
    a_log,
    d_skip,
    norm_gain,
    w_out,
    ssm_state,
    conv_x_state,
    conv_bc_state,
    slot,
    lengths,
    accepted,
):
    rows, steps, width_part = hidden.shape
    width = w_zx.shape[0]
    chans = w_zx.shape[2]
    myself = lax.axis_index("req")
    peers = lax.axis_size("req")
    send_order, to_pool, back_order, home, request = routes(slot, rows, myself, peers)
    counted = jnp.minimum(accepted, lengths)
    hit = jnp.arange(slot.shape[0], dtype=jnp.int32)[None, :] == request[:, None]
    my_counted = jnp.sum(jnp.where(hit, counted[None, :], 0), axis=1, dtype=jnp.int32)

    outgoing = jnp.take(hidden, send_order, axis=0)
    arrived = lax.all_to_all(outgoing, "req", split_axis=0, concat_axis=0, tiled=True)
    pooled = jnp.take(arrived, to_pool, axis=0)
    tokens = lax.all_gather(pooled, "head", axis=2, tiled=True).reshape(rows * steps, width)
    zx = jnp.dot(tokens, w_zx.reshape(width, 2 * chans), preferred_element_type=f32).astype(bf16)
    bcdt = jnp.dot(tokens, jnp.concatenate([w_bc, w_dt], axis=1), preferred_element_type=f32).astype(bf16)
    g, squares, new_state, new_conv_x, new_conv_bc = core(
        my_counted,
        zx,
        bcdt,
        ssm_state,
        conv_x_state,
        conv_bc_state,
        conv_x_w,
        conv_bc_w,
        jnp.stack([dt_bias, a_log, d_skip]),
        norm_gain[None, :],
        4,
    )
    partial_out = jnp.dot(g, w_out, preferred_element_type=f32).astype(bf16)
    summed = lax.psum_scatter(partial_out, "head", scatter_dimension=1, tiled=True)
    meansq = lax.psum(squares, "head") / (chans * lax.axis_size("head"))
    result = (summed.astype(f32) * lax.rsqrt(meansq + 1e-05)).astype(bf16).reshape(rows, steps, width_part)
    back = lax.all_to_all(jnp.take(result, back_order, axis=0), "req", split_axis=0, concat_axis=0, tiled=True)
    mine = jnp.take(back, home, axis=0)
    my_lengths = lax.dynamic_slice_in_dim(lengths, myself * rows, rows, 0)
    valid = jnp.arange(steps, dtype=jnp.int32)[None, :] < my_lengths[:, None]
    out = jnp.where(valid[..., None], mine, jnp.zeros((), bf16))
    return (out, new_state, new_conv_x, new_conv_bc)


def solution(mesh):
    in_specs = (
        P("req", None, "head"),
        P(None, None, "head"),
        P(),
        P(None, "head"),
        P(None, "head"),
        P(),
        P("head"),
        P("head"),
        P("head"),
        P("head"),
        P("head", None),
        P("req", "head", None, None),
        P("req", None, "head"),
        P("req", None, None),
        P(),
        P(),
        P(),
    )
    out_specs = (
        P("req", None, "head"),
        P("req", "head", None, None),
        P("req", None, "head"),
        P("req", None, None),
    )
    return jax.shard_map(
        per_device, mesh=mesh, in_specs=in_specs, out_specs=out_specs, check_vma=False
    )
```

time: 554 us -> 186 us (0.34); the launches traced: 544 us -> 186 us
  waiting for transfers between devices: 278 us -> 67.7 us
  local copies, waits for them, and re-layouts: 87.3 us -> 20.1 us
  matrix products: 68 us -> 13.2 us
  other arithmetic: 50.7 us -> 7.25 us
  Pallas kernels: 0 us -> 24.5 us
  starting transfers between devices: 28.4 us -> 8.9 us
  blocking collectives: 16.9 us -> 29.8 us
    all_to_all x6 -> x2, waiting for transfers between devices: 199 us -> 16.8 us  [the longest x1 8.83 us: per_device(): lax.all_to_all(outgoing, 'req', split_axis=0, concat_axis=0, tiled=True)]
    dot_general x6 -> x3, matrix products: 68 us -> 13.2 us  [the longest x1 8.65 us: per_device(): jnp.dot(tokens, w_zx.reshape(width, 2 * chans), preferred_element_type=f32)]
    reduce_scatter x1, waiting for transfers between devices: 69.6 us -> 18.1 us  [per_device(): lax.psum_scatter(partial_out, 'head', scatter_dimension=1, tiled=True)]
    gather x21 -> x4, local copies, waits for them, and re-layouts: 47.8 us -> 2.32 us  [the longest x1 0.58 us: per_device(): jnp.take(result, back_order, axis=0)]
    select_n x14 -> x9, other arithmetic: 29.4 us -> 3.73 us  [the longest x1 0.97 us: per_device(): out = jnp.where(valid[..., None], mine, jnp.zeros((), bf16))]
    pallas_call x0 -> x1, Pallas kernels: none -> 24.5 us  [core(): pl.pallas_call(functools.partial(core_kernel, group), grid_spec=pltpu.Pre...]
    all_gather x1, waiting for transfers between devices: 8.59 us -> 32.8 us  [per_device(): lax.all_gather(pooled, 'head', axis=2, tiled=True)]
    all_to_all x6 -> x2, starting transfers between devices: 28.3 us -> 8.82 us  [the longest x1 5.17 us: per_device(): lax.all_to_all(outgoing, 'req', split_axis=0, concat_axis=0, tiled=True)]
  transfers between devices with their start and end apart: 8 -> 4, of which waited for: 5 -> 4; matrix products, arithmetic and copies ran while one was open for 33% -> 8% of each run, Pallas kernels for 0% -> 0%
where the time goes in v1:
time: 186 us
  waiting for transfers between devices  67.7 us (36%)
  blocking collectives  29.8 us (16%)
  Pallas kernels  24.5 us (13%)
  local copies, waits for them, and re-layouts  20.1 us (11%)
  between operations  14.5 us (8%)
  matrix products  13.2 us (7%)
  starting transfers between devices  8.9 us (5%)
  other arithmetic  7.25 us (4%)
    all_gather x1, waiting for transfers between devices, per_device(): lax.all_gather(pooled, 'head', axis=2, tiled=True)  32.8 us
    psum x1, blocking collectives, per_device(): meansq = lax.psum(squares, 'head') / (chans * lax.axis_size('head'))  29.8 us
    pallas_call x1, Pallas kernels, core(): pl.pallas_call(functools.partial(core_kernel, group), grid_spec=pltpu.Pre...  24.5 us
    reduce_scatter x1, waiting for transfers between devices, per_device(): lax.psum_scatter(partial_out, 'head', scatter_dimension=1, tiled=True)  18.1 us
    unnamed x60, local copies, waits for them, and re-layouts  16.6 us
    all_to_all x1, waiting for transfers between devices, per_device(): lax.all_to_all(outgoing, 'req', split_axis=0, concat_axis=0, tiled=True)  8.83 us
    dot_general x1, matrix products, per_device(): jnp.dot(tokens, w_zx.reshape(width, 2 * chans), preferred_element_type=f32)  8.65 us
    all_to_all x1, waiting for transfers between devices, per_device(): lax.all_to_all(jnp.take(result, back_order, axis=0), 'req', split_axis=0,...  8 us
  transfers between devices with their start and end apart: 4, of which 4 were waited for; matrix products, arithmetic and copies ran while one was open for 8% of the time, Pallas kernels for 0%

profile of v1, /device:TPU:0, one launch (start us, length us, event | category | flops | bytes accessed | tf_op | source)
XLA Modules:
  0.0 185.9 jit_solution(4917421814717915595)
XLA Ops:
  7.2 0.0 copy-start
  7.2 0.0 copy-start.12
  7.2 0.8 reshape.145
  8.0 0.3 convert_reduce_fusion
  8.3 0.5 compare_and_fusion
  8.9 0.1 select_reduce_fusion.2
  9.0 0.4 copy-done.20
  9.5 0.6 gather_fusion
  10.1 0.9 broadcast_select_fusion.2
  11.0 5.2 %all-to-all-start = ((bf16[32,16,512]{2,1,0:T(8,128)(2,1)}), bf16[32,16,512]{2,1,0:T(8,128)(2,1)S(1)}, u32[]{:S(2)}, u32[]{:S(2)}) async-start(bf16[32,16,512]{2,1,0:T(8,128)(2,1)} %broadcast_select_fusion.2), calls=%async_computation | async-start | bytes 1048576 | tf_op jit(solution)/shard_map/all_to_all | solution.py:252
  16.1 0.0 all-gather.2.cloned.1.call-start
  16.2 0.1 broadcast_add_fusion
  16.3 0.1 add.70
  16.4 0.2 fusion.8
  16.6 0.5 copy-done.22
  17.1 8.8 %all-to-all-done = bf16[32,16,512]{2,1,0:T(8,128)(2,1)S(1)} async-done(((bf16[32,16,512]{2,1,0:T(8,128)(2,1)}), bf16[32,16,512]{2,1,0:T(8,128)(2,1)S(1)}, u32[]{:S(2)}, u32[]{:S(2)}) %all-to-all-start) | async-done | bytes 524320 | tf_op jit(solution)/shard_map/all_to_all | solution.py:252
  25.9 0.6 gather_fusion.1
  26.5 0.9 broadcast_select_fusion.1
  27.4 0.0 all-gather.2.cloned.1.call-update
  27.4 0.0 reduce-scatter.2.cloned.1.call-start
  27.5 0.0 copy-start.11
  27.5 0.0 copy-start.9
  27.5 0.0 copy-start.10
  27.5 0.0 copy-start.14
  27.5 0.0 copy-start.15
  27.5 0.0 copy-start.17
  27.5 0.0 copy-start.18
  27.5 0.0 copy-start.19
  27.6 10.4 %copy.45 = bf16[256,8,2,1024]{3,1,2,0:T(8,128)(2,1)} copy(bf16[256,8,2,1024]{3,2,1,0:T(2,128)(2,1)} %bitcast.17) | data formatting | bytes 16777216
  37.9 1.0 copy.39
  39.0 0.3 copy.41.cx_ref
  39.2 0.1 copy.42.cbc_ref
  39.3 0.0 copy-done.17
  39.4 0.0 copy-done.18
  39.4 0.7 select_reduce_fusion.counted_ref
  40.1 32.8 %all-gather.2.cloned.1.call-done = bf16[32,16,2048]{2,1,0:T(8,128)(2,1)} async-done(((bf16[32,16,512]{2,1,0:T(8,128)(2,1)}), bf16[32,16,2048]{2,1,0:T(8,128)(2,1)}) %all-gather.2.cloned.1.call-update) | async-done | bytes 2097168 | tf_op jit(solution)/shard_map/all_gather | solution.py:254
  72.9 8.7 %convolution_convert_fusion.1.zx_ref = bf16[512,2048]{1,0:T(8,128)(2,1)S(1)} fusion(bf16[512,2048]{1,0:T(8,128)(2,1)} %bitcast.23, bf16[2048,2048]{1,0:T(8,128)(2,1)} %bitcast.18), kind=kOutput, calls=%fused_computation.5 | convolution fusion | flops 4296015872 | bytes 12582912 | tf_op jit(solution)/shard_map/dot_general | solution.py:255
  81.6 0.0 copy-start.5
  81.6 0.0 copy-start.6
  81.6 0.8 fusion.4
  82.4 0.2 copy.40.bcdt_ref
  82.6 0.0 copy-start.4
  82.7 0.7 copy-done.4
  83.4 0.7 copy-done.7
  84.1 24.5 %core.1 = (bf16[512,1024]{1,0:T(8,128)(2,1)S(1)}, f32[512,1]{1,0:T(8,128)S(1)}, f32[32,16,64,128]{3,2,1,0:T(8,128)}, f32[32,3,1024]{2,1,0:T(4,128)S(1)}, f32[32,3,256]{2,1,0:T(4,128)S(1)}) custom-call(s32[32]{0:T(128)S(1)} %copy-done.7, bf16[512,2048]{1,0:T(8,128)(2,1)S(1)} %convolution_convert_fusion.1.zx_ref, bf16[512,272]{1,0:T(8,128)(2,1)S(1)} %copy.40.bcdt_ref, ...), custom_call_target="tpu_custom_call" | custom-call | tf_op jit(solution)/shard_map/core/pallas_call | solution.py:162
  108.5 0.8 copy-done.2
  109.3 3.7 %convolution_convert_fusion = bf16[512,2048]{1,0:T(8,128)(2,1)} fusion(bf16[512,1024]{1,0:T(8,128)(2,1)S(1)} %get-tuple-element.10, bf16[1024,2048]{1,0:T(8,128)(2,1)S(1)} %copy-done.24), kind=kOutput, calls=%fused_computation.4 | convolution fusion | flops 2148532224 | bytes 7340032 | tf_op jit(solution)/shard_map/dot_general | solution.py:270
  113.0 0.0 reduce-scatter.2.cloned.1.call-update
  113.1 0.1 dynamic_slice.10
  113.2 0.1 select_reduce_fusion.1
  113.3 29.8 %psum.7 = f32[512,1]{1,0:T(8,128)S(1)} all-reduce(f32[512,1]{1,0:T(8,128)S(1)} %get-tuple-element.11), channel_id=1, replica_groups=mesh['req'=8,'head'=4] {'head'}, use_global_device_ids=true, to_apply=%region_6.8 | all-reduce | flops 512 | bytes 4096 | tf_op jit(solution)/shard_map/psum | solution.py:272
  143.2 0.2 rsqrt_reduce_fusion
  143.3 18.1 %reduce-scatter.2.cloned.1.call-done = bf16[512,512]{1,0:T(8,128)(2,1)} async-done(((bf16[512,2048]{1,0:T(8,128)(2,1)}), bf16[512,512]{1,0:T(8,128)(2,1)}) %reduce-scatter.2.cloned.1.call-update) | async-done | bytes 524304 | tf_op jit(solution)/shard_map/reduce_scatter | solution.py:271
  161.4 1.2 multiply_convert_fusion
  162.6 0.0 copy-start.1
  162.6 0.6 gather_fusion.2
  163.2 0.9 broadcast_select_fusion
  164.1 3.6 %all-to-all-start.1 = ((bf16[32,16,512]{2,1,0:T(8,128)(2,1)}), bf16[32,16,512]{2,1,0:T(8,128)(2,1)S(1)}, u32[]{:S(2)}, u32[]{:S(2)}) async-start(bf16[32,16,512]{2,1,0:T(8,128)(2,1)} %broadcast_select_fusion), calls=%async_computation.2 | async-start | bytes 1048576 | tf_op jit(solution)/shard_map/all_to_all | solution.py:274
  167.8 0.1 iota_compare_fusion.4
  167.9 1.0 copy.43
  168.9 0.7 copy.44
  169.5 8.0 %all-to-all-done.1 = bf16[32,16,512]{2,1,0:T(8,128)(2,1)S(1)} async-done(((bf16[32,16,512]{2,1,0:T(8,128)(2,1)}), bf16[32,16,512]{2,1,0:T(8,128)(2,1)S(1)}, u32[]{:S(2)}, u32[]{:S(2)}) %all-to-all-start.1) | async-done | bytes 524320 | tf_op jit(solution)/shard_map/all_to_all | solution.py:274
  177.5 0.6 gather_fusion.3
  178.1 1.0 select_select_fusion
  (50 shorter events, 0.2 us)
Async XLA Ops:
  7.2 2.3 %copy-start = (bf16[32,16,512]{2,1,0:T(8,128)(2,1)S(1)}, bf16[32,16,512]{2,1,0:T(8,128)(2,1)}, u32[]{:S(2)}) copy-start(bf16[32,16,512]{2,1,0:T(8,128)(2,1)} %param.19) | copy-start | bytes 1572868
  7.2 9.2 %copy-start.12 = (s32[256]{0:T(256)S(1)}, s32[256]{0:T(256)}, u32[]{:S(2)}) copy-start(s32[256]{0:T(256)} %param.33) | copy-start | bytes 3076
  8.9 0.6 copy-start.20
  11.0 14.9 %all-to-all-start = ((bf16[32,16,512]{2,1,0:T(8,128)(2,1)}), bf16[32,16,512]{2,1,0:T(8,128)(2,1)S(1)}, u32[]{:S(2)}, u32[]{:S(2)}) async-start(bf16[32,16,512]{2,1,0:T(8,128)(2,1)} %broadcast_select_fusion.2), calls=%async_computation | async-start | bytes 1048576 | tf_op jit(solution)/shard_map/all_to_all | solution.py:252
  16.1 56.7 %all-gather.2.cloned.1.call-start = ((), (), s32[]{:S(2)}) async-start(), calls=%async_computation.3 | async-start | bytes 2621440 | tf_op jit(solution)/shard_map/all_gather | solution.py:254
  16.5 0.5 copy-start.22
  27.4 134.0 %reduce-scatter.2.cloned.1.call-start = ((), (), s32[]{:S(2)}) async-start(), calls=%async_computation.4 | async-start | bytes 2621440 | tf_op jit(solution)/shard_map/reduce_scatter | solution.py:271
  27.5 10.5 %copy-start.11 = (bf16[2048,16]{0,1:T(8,128)(2,1)S(1)}, bf16[2048,16]{0,1:T(8,128)(2,1)}, u32[]{:S(2)}) copy-start(bf16[2048,16]{0,1:T(8,128)(2,1)} %param.22) | copy-start | bytes 196612
  27.5 11.5 %copy-start.9 = (f32[32,3,1024]{2,0,1:T(8,128)S(1)}, f32[32,3,1024]{2,0,1:T(8,128)}, u32[]{:S(2)}) copy-start(f32[32,3,1024]{2,0,1:T(8,128)} %param.31) | copy-start | bytes 1179652
  27.5 11.7 %copy-start.10 = (f32[32,3,256]{2,0,1:T(8,128)S(1)}, f32[32,3,256]{2,0,1:T(8,128)}, u32[]{:S(2)}) copy-start(f32[32,3,256]{2,0,1:T(8,128)} %param.32) | copy-start | bytes 294916
  27.5 11.8 %copy-start.14 = (s32[256]{0:T(256)S(1)}, s32[256]{0:T(256)}, u32[]{:S(2)}) copy-start(s32[256]{0:T(256)} %param.35) | copy-start | bytes 3076
  27.5 11.8 %copy-start.15 = (s32[256]{0:T(256)S(1)}, s32[256]{0:T(256)}, u32[]{:S(2)}) copy-start(s32[256]{0:T(256)} %param.34) | copy-start | bytes 3076
  27.5 11.8 %copy-start.17 = (f32[16]{0:T(128)S(1)}, f32[16]{0:T(128)}, u32[]{:S(2)}) copy-start(f32[16]{0:T(128)} %param.27) | copy-start | bytes 196
  27.5 11.8 %copy-start.18 = (f32[16]{0:T(128)S(1)}, f32[16]{0:T(128)}, u32[]{:S(2)}) copy-start(f32[16]{0:T(128)} %param.26) | copy-start | bytes 196
  27.5 11.8 %copy-start.19 = (f32[16]{0:T(128)S(1)}, f32[16]{0:T(128)}, u32[]{:S(2)}) copy-start(f32[16]{0:T(128)} %param.25) | copy-start | bytes 196
  72.9 8.7 %copy-start.8 = (bf16[2048,16]{1,0:T(8,128)(2,1)S(1)}, bf16[2048,16]{1,0:T(8,128)(2,1)}, u32[]{:S(2)}) copy-start(bf16[2048,16]{1,0:T(8,128)(2,1)} %copy.39) | copy-start | bytes 196612
  72.9 8.7 %copy-start.25 = (bf16[32,16,2048]{2,1,0:T(8,128)(2,1)S(1)}, bf16[32,16,2048]{2,1,0:T(8,128)(2,1)}, u32[]{:S(2)}) copy-start(bf16[32,16,2048]{2,1,0:T(8,128)(2,1)} %all-gather.2.cloned.1.call-done) | copy-start | bytes 6291460
  72.9 8.7 %copy-start.26 = (bf16[2048,256]{1,0:T(8,128)(2,1)S(1)}, bf16[2048,256]{1,0:T(8,128)(2,1)}, u32[]{:S(2)}) copy-start(bf16[2048,256]{1,0:T(8,128)(2,1)} %param.21) | copy-start | bytes 3145732
  81.6 1.1 copy-start.5
  81.6 1.1 copy-start.6
  82.6 0.8 copy-start.4
  83.4 0.7 copy-start.7
  84.1 25.3 %copy-start.24 = (bf16[1024,2048]{1,0:T(8,128)(2,1)S(1)}, bf16[1024,2048]{1,0:T(8,128)(2,1)}, u32[]{:S(2)}) copy-start(bf16[1024,2048]{1,0:T(8,128)(2,1)} %param.29) | copy-start | bytes 12582916
  108.5 0.8 copy-start.2
  109.3 3.7 %copy-start.16 = (s32[256]{0:T(256)S(1)}, s32[256]{0:T(256)}, u32[]{:S(2)}) copy-start(s32[256]{0:T(256)} %param.34) | copy-start | bytes 3076
  109.3 3.8 %copy-start.23 = (s32[32]{0:T(128)S(1)}, s32[32]{0:T(128)}, u32[]{:S(2)}) copy-start(s32[32]{0:T(128)} %copy-done.22) | copy-start | bytes 388
  113.0 54.8 %copy-start.21 = (s32[32]{0:T(128)S(1)}, s32[32]{0:T(128)}, u32[]{:S(2)}) copy-start(s32[32]{0:T(128)} %copy-done.20) | copy-start | bytes 388
  113.0 54.9 %copy-start.3 = (f32[32,3,1024]{2,1,0:T(4,128)S(1)}, f32[32,3,1024]{2,1,0:T(4,128)}, u32[]{:S(2)}) copy-start(f32[32,3,1024]{2,1,0:T(4,128)} %copy-done.2) | copy-start | bytes 1179652
  143.3 34.8 %copy-start.13 = (pred[32]{0:T(512)(128)(4,1)S(1)}, pred[32]{0:T(512)(128)(4,1)}, u32[]{:S(2)}) copy-start(pred[32]{0:T(512)(128)(4,1)} %get-tuple-element.33) | copy-start | bytes 100
  162.6 16.5 %copy-start.1 = (bf16[32,16,512]{2,1,0:T(8,128)(2,1)S(1)}, bf16[32,16,512]{2,1,0:T(8,128)(2,1)}, u32[]{:S(2)}) copy-start(bf16[32,16,512]{2,1,0:T(8,128)(2,1)} %param.19) | copy-start | bytes 1572868
  164.1 13.4 %all-to-all-start.1 = ((bf16[32,16,512]{2,1,0:T(8,128)(2,1)}), bf16[32,16,512]{2,1,0:T(8,128)(2,1)S(1)}, u32[]{:S(2)}, u32[]{:S(2)}) async-start(bf16[32,16,512]{2,1,0:T(8,128)(2,1)} %broadcast_select_fusion), calls=%async_computation.2 | async-start | bytes 1048576 | tf_op jit(solution)/shard_map/all_to_all | solution.py:274
Sparse Core Ops, SparseCore 0:
  27.5 45.2 all-gather.1
  113.2 48.1 reduce-scatter.1

commit v2 on v1

--- a/solution.py
+++ b/solution.py
@@ -47,6 +47,7 @@
 
 def core_kernel(
     group,
+    offset,
     counted_ref,
     zx_ref,
     bcdt_ref,
@@ -57,20 +58,15 @@
     cbw_ref,
     heads_ref,
     gain_ref,
-    g_ref,
-    sq_ref,
-    new_state_ref,
-    ncx_ref,
-    ncbc_ref,
-    xwin,
-    bcwin,
+    *refs,
 ):
+    (g_ref, sq_ref, new_state_ref, ncx_ref, ncbc_ref, xwin, bcwin) = refs[-7:]
     heads, headdim, nstate = state_ref.shape[1:]
     chans = heads * headdim
     tokens = zx_ref.shape[0]
     steps = tokens // group
     tail = cx_ref.shape[1]
-    first = pl.program_id(0) * group
+    first = (pl.program_id(0) + offset) * group
 
     def count_of(r):
         return counted_ref[first + r]
@@ -146,41 +142,47 @@
     g_ref[...] = (gated * gain_ref[...]).astype(bf16)
 
 
-def core(counted, zx, bcdt, states, cx, cbc, cxw, cbw, head_params, gain, group):
+def core(counted, zx, bcdt, states, cx, cbc, cxw, cbw, head_params, gain, group, chunk, chunks, done):
     rows, heads, headdim, nstate = states.shape
     chans = heads * headdim
-    steps = zx.shape[0] // rows
+    steps = zx.shape[0] * chunks // rows
     tail = cx.shape[1]
     tokens = group * steps
+    calls = rows // group // chunks
+    offset = chunk * calls
 
     def step_block(*shape):
         return pl.BlockSpec(shape, lambda i, c: (i,) + (0,) * (len(shape) - 1))
 
+    def pool_block(*shape):
+        return pl.BlockSpec(shape, lambda i, c: (i + offset,) + (0,) * (len(shape) - 1))
+
     def whole(a):
         return pl.BlockSpec(a.shape, lambda i, c: (0,) * a.ndim)
 
     return pl.pallas_call(
-        functools.partial(core_kernel, group),
+        functools.partial(core_kernel, group, offset),
         grid_spec=pltpu.PrefetchScalarGridSpec(
             num_scalar_prefetch=1,
-            grid=(rows // group,),
+            grid=(calls,),
             in_specs=[
                 step_block(tokens, 2 * chans),
                 step_block(tokens, bcdt.shape[1]),
-                step_block(group, heads, headdim, nstate),
-                step_block(group, tail, chans),
-                step_block(group, tail, 2 * nstate),
+                pool_block(group, heads, headdim, nstate),
+                pool_block(group, tail, chans),
+                pool_block(group, tail, 2 * nstate),
                 whole(cxw),
                 whole(cbw),
                 whole(head_params),
                 whole(gain),
-            ],
+            ]
+            + [pl.BlockSpec(memory_space=pl.ANY)] * len(done),
             out_specs=[
                 step_block(tokens, chans),
                 step_block(tokens, 1),
-                step_block(group, heads, headdim, nstate),
-                step_block(group, tail, chans),
-                step_block(group, tail, 2 * nstate),
+                pool_block(group, heads, headdim, nstate),
+                pool_block(group, tail, chans),
+                pool_block(group, tail, 2 * nstate),
             ],
             scratch_shapes=[
                 pltpu.VMEM((group, 8 + steps, chans), f32),
@@ -188,15 +190,21 @@
             ],
         ),
         out_shape=[
-            jax.ShapeDtypeStruct((rows * steps, chans), bf16),
-            jax.ShapeDtypeStruct((rows * steps, 1), f32),
+            jax.ShapeDtypeStruct((zx.shape[0], chans), bf16),
+            jax.ShapeDtypeStruct((zx.shape[0], 1), f32),
             jax.ShapeDtypeStruct(states.shape, f32),
             jax.ShapeDtypeStruct(cx.shape, f32),
             jax.ShapeDtypeStruct(cbc.shape, f32),
         ],
-        compiler_params=pltpu.CompilerParams(vmem_limit_bytes=48 * 1024 * 1024),
+        input_output_aliases={10 + k: 2 + k for k in range(len(done))},
+        compiler_params=pltpu.CompilerParams(vmem_limit_bytes=40 * 1024 * 1024),
+        cost_estimate=pl.CostEstimate(
+            flops=2 * zx.shape[0] * chans * nstate * 8,
+            bytes_accessed=8 * (rows // chunks) * chans * nstate,
+            transcendentals=zx.shape[0] * chans * 2,
+        ),
         name="core",
-    )(counted, zx, bcdt, states, cx, cbc, cxw, cbw, head_params, gain)
+    )(counted, zx, bcdt, states, cx, cbc, cxw, cbw, head_params, gain, *done)
 
 
 def routes(slot, rows, myself, peers):
@@ -251,26 +259,51 @@
     outgoing = jnp.take(hidden, send_order, axis=0)
     arrived = lax.all_to_all(outgoing, "req", split_axis=0, concat_axis=0, tiled=True)
     pooled = jnp.take(arrived, to_pool, axis=0)
-    tokens = lax.all_gather(pooled, "head", axis=2, tiled=True).reshape(rows * steps, width)
-    zx = jnp.dot(tokens, w_zx.reshape(width, 2 * chans), preferred_element_type=f32).astype(bf16)
-    bcdt = jnp.dot(tokens, jnp.concatenate([w_bc, w_dt], axis=1), preferred_element_type=f32).astype(bf16)
-    g, squares, new_state, new_conv_x, new_conv_bc = core(
-        my_counted,
-        zx,
-        bcdt,
-        ssm_state,
-        conv_x_state,
-        conv_bc_state,
-        conv_x_w,
-        conv_bc_w,
-        jnp.stack([dt_bias, a_log, d_skip]),
-        norm_gain[None, :],
-        4,
-    )
-    partial_out = jnp.dot(g, w_out, preferred_element_type=f32).astype(bf16)
-    summed = lax.psum_scatter(partial_out, "head", scatter_dimension=1, tiled=True)
-    meansq = lax.psum(squares, "head") / (chans * lax.axis_size("head"))
-    result = (summed.astype(f32) * lax.rsqrt(meansq + 1e-05)).astype(bf16).reshape(rows, steps, width_part)
+    chunks = 2
+    part = rows // chunks
+    flat_zx = w_zx.reshape(width, 2 * chans)
+    w_bcdt = jnp.concatenate([w_bc, w_dt], axis=1)
+    head_params = jnp.stack([dt_bias, a_log, d_skip])
+    hold = lax.optimization_barrier
+
+    gathered = []
+    for c in range(chunks):
+        piece = pooled[c * part : (c + 1) * part]
+        if c > 0:
+            gathered[-1], piece = hold((gathered[-1], piece))
+        gathered.append(lax.all_gather(piece, "head", axis=2, tiled=True))
+    done, squares, summed = (), [], []
+    for c in range(chunks):
+        tokens = gathered[c].reshape(part * steps, width)
+        zx = jnp.dot(tokens, flat_zx, preferred_element_type=f32).astype(bf16)
+        bcdt = jnp.dot(tokens, w_bcdt, preferred_element_type=f32).astype(bf16)
+        g, sq, *done = core(
+            my_counted,
+            zx,
+            bcdt,
+            ssm_state,
+            conv_x_state,
+            conv_bc_state,
+            conv_x_w,
+            conv_bc_w,
+            head_params,
+            norm_gain[None, :],
+            4,
+            c,
+            chunks,
+            done,
+        )
+        squares.append(sq)
+        shares = jnp.dot(g, w_out, preferred_element_type=f32).astype(bf16)
+        if c > 0:
+            summed[-1], shares = hold((summed[-1], shares))
+        summed.append(lax.psum_scatter(shares, "head", scatter_dimension=1, tiled=True))
+    new_state, new_conv_x, new_conv_bc = done
+    square = jnp.concatenate(squares, axis=0).reshape(-1, 128)
+    total = jnp.sum(lax.all_gather(square, "head", axis=0), axis=0).reshape(rows * steps, 1)
+    meansq = total / (chans * lax.axis_size("head"))
+    full = jnp.concatenate(summed, axis=0).astype(f32)
+    result = (full * lax.rsqrt(meansq + 1e-05)).astype(bf16).reshape(rows, steps, width_part)
     back = lax.all_to_all(jnp.take(result, back_order, axis=0), "req", split_axis=0, concat_axis=0, tiled=True)
     mine = jnp.take(back, home, axis=0)
     my_lengths = lax.dynamic_slice_in_dim(lengths, myself * rows, rows, 0)

time: 186 us -> 169 us (0.909)
  blocking collectives: 29.8 us -> 11.9 us
  matrix products: 13.2 us -> 19.3 us
  waiting for transfers between devices: 67.7 us -> 63 us
  Pallas kernels: 24.5 us -> 27.9 us
  local copies, waits for them, and re-layouts: 20.1 us -> 17.4 us
    psum x1 -> x0, blocking collectives: 29.8 us -> none  [per_device(): meansq = lax.psum(squares, 'head') / (chans * lax.axis_size('head'))]
    all_gather x0 -> x1, blocking collectives: none -> 11.9 us  [per_device(): lax.all_gather(square, 'head', axis=0)]
    dot_general x3 -> x6, matrix products: 13.2 us -> 19.3 us  [the longest x2 12.3 us: per_device(): zx = jnp.dot(tokens, flat_zx, preferred_element_type=f32).astype(bf16)]
    all_gather x1 -> x2, waiting for transfers between devices: 32.8 us -> 27.4 us  [per_device(): gathered.append(lax.all_gather(piece, 'head', axis=2, tiled=True))]
    unnamed x60 -> x40, local copies, waits for them, and re-layouts: 16.6 us -> 12.6 us
    pallas_call x1 -> x2, Pallas kernels: 24.5 us -> 27.9 us  [core(): pl.pallas_call(functools.partial(core_kernel, group, offset), grid_spec=p...]
    reduce_scatter x1 -> x2, waiting for transfers between devices: 18.1 us -> 17.9 us  [per_device(): lax.psum_scatter(shares, 'head', scatter_dimension=1, tiled=True)]
  transfers between devices with their start and end apart: 4 -> 6, of which waited for: 4 -> 5; matrix products, arithmetic and copies ran while one was open for 8% -> 19% of each run, Pallas kernels for 0% -> 17%
where the time goes in v2:
time: 169 us
  waiting for transfers between devices  63 us (37%)
  Pallas kernels  27.9 us (17%)
  matrix products  19.3 us (11%)
  local copies, waits for them, and re-layouts  17.4 us (10%)
  between operations  14.2 us (8%)
  blocking collectives  11.9 us (7%)
  starting transfers between devices  9.18 us (5%)
  other arithmetic  6 us (4%)
    pallas_call x2, Pallas kernels, core(): pl.pallas_call(functools.partial(core_kernel, group, offset), grid_spec=p...  27.9 us
    all_gather x2, waiting for transfers between devices, per_device(): gathered.append(lax.all_gather(piece, 'head', axis=2, tiled=True))  27.4 us
    reduce_scatter x2, waiting for transfers between devices, per_device(): lax.psum_scatter(shares, 'head', scatter_dimension=1, tiled=True)  17.9 us
    unnamed x40, local copies, waits for them, and re-layouts  12.6 us
    dot_general x2, matrix products, per_device(): zx = jnp.dot(tokens, flat_zx, preferred_element_type=f32).astype(bf16)  12.3 us
    all_gather x1, blocking collectives, per_device(): lax.all_gather(square, 'head', axis=0)  11.9 us
    all_to_all x1, waiting for transfers between devices, per_device(): lax.all_to_all(outgoing, 'req', split_axis=0, concat_axis=0, tiled=True)  9.66 us
    all_to_all x1, waiting for transfers between devices, per_device(): lax.all_to_all(jnp.take(result, back_order, axis=0), 'req', split_axis=0,...  8.01 us
  transfers between devices with their start and end apart: 6, of which 5 were waited for; matrix products, arithmetic and copies ran while one was open for 19% of the time, Pallas kernels for 17%

profile of v2, /device:TPU:0, one launch (start us, length us, event | category | flops | bytes accessed | tf_op | source)
XLA Modules:
  0.0 168.9 jit_solution(4085969481192558714)
XLA Ops:
  7.2 0.0 copy-start
  7.3 0.9 reshape.171
  8.2 0.3 convert_reduce_fusion
  8.5 0.1 broadcast_add_fusion
  8.5 0.1 add.76
  8.6 0.9 fusion.2
  9.5 0.1 select_reduce_fusion.1
  9.6 0.1 select_reduce_fusion.2
  9.8 0.6 gather_fusion
  10.4 0.9 broadcast_select_fusion.2
  11.3 5.2 %all-to-all-start = ((bf16[32,16,512]{2,1,0:T(8,128)(2,1)}), bf16[32,16,512]{2,1,0:T(8,128)(2,1)S(1)}, u32[]{:S(2)}, u32[]{:S(2)}) async-start(bf16[32,16,512]{2,1,0:T(8,128)(2,1)} %broadcast_select_fusion.2), calls=%async_computation | async-start | bytes 1048576 | tf_op jit(solution)/shard_map/all_to_all | solution.py:260
  16.5 0.0 all-gather.3.cloned.1.call-start
  16.5 9.7 %all-to-all-done = bf16[32,16,512]{2,1,0:T(8,128)(2,1)S(1)} async-done(((bf16[32,16,512]{2,1,0:T(8,128)(2,1)}), bf16[32,16,512]{2,1,0:T(8,128)(2,1)S(1)}, u32[]{:S(2)}, u32[]{:S(2)}) %all-to-all-start) | async-done | bytes 524320 | tf_op jit(solution)/shard_map/all_to_all | solution.py:260
  26.2 0.6 gather_fusion.1
  26.8 0.1 broadcast_select_fusion.1
  26.9 0.8 fusion.7
  27.7 0.0 all-gather.3.cloned.1.call-update
  27.8 0.0 all-gather.5.cloned.1.call-start
  27.8 27.4 %all-gather.3.cloned.1.call-done = bf16[16,16,2048]{2,1,0:T(8,128)(2,1)} async-done(((bf16[16,16,512]{2,1,0:T(8,128)(2,1)}), bf16[16,16,2048]{2,1,0:T(8,128)(2,1)}) %all-gather.3.cloned.1.call-update) | async-done | bytes 1048592 | tf_op jit(solution)/shard_map/all_gather | solution.py:274
  55.2 0.0 all-gather.5.cloned.1.call-update
  55.2 0.0 reduce-scatter.3.cloned.1.call-start
  55.3 0.1 copy.67.cbc_ref
  55.4 0.3 copy.64
  55.7 0.3 copy.66.cx_ref
  56.0 0.0 copy-start.8
  56.0 0.0 copy-start.9
  56.0 0.0 copy-start.15
  56.0 10.3 %copy.75 = bf16[256,8,2,1024]{3,1,2,0:T(8,128)(2,1)} copy(bf16[256,8,2,1024]{3,2,1,0:T(2,128)(2,1)} %bitcast.26) | data formatting | bytes 16777216
  66.3 0.2 select_reduce_fusion.counted_ref
  66.5 0.7 convolution_convert_fusion.5
  67.2 0.2 copy.65.bcdt_ref
  67.4 0.0 copy-start.2
  67.4 0.0 copy-start.3
  67.4 0.0 copy-start.4
  67.4 6.1 %convolution_convert_fusion.3.zx_ref = bf16[256,2048]{1,0:T(8,128)(2,1)S(1)} fusion(bf16[256,2048]{1,0:T(8,128)(2,1)} %bitcast.36, bf16[2048,2048]{1,0:T(8,128)(2,1)} %bitcast.27), kind=kOutput, calls=%fused_computation.7 | convolution fusion | flops 2148007936 | bytes 10485760 | tf_op jit(solution)/shard_map/dot_general | solution.py:278
  73.6 14.0 %core.2 = (bf16[256,1024]{1,0:T(8,128)(2,1)S(1)}, f32[256,1]{1,0:T(8,128)S(1)}, f32[32,16,64,128]{3,2,1,0:T(8,128)}, f32[32,3,1024]{2,1,0:T(4,128)S(1)}, f32[32,3,256]{2,1,0:T(4,128)S(1)}) custom-call(s32[32]{0:T(128)S(1)} %select_reduce_fusion.counted_ref, bf16[256,2048]{1,0:T(8,128)(2,1)S(1)} %convolution_convert_fusion.3.zx_ref, ...), custom_call_target="tpu_custom_call" | custom-call | flops 536870912 | bytes 16777216 | tf_op jit(solution)/shard_map/core/pallas_call | solution.py:163
  87.5 2.2 %convolution_convert_fusion.1 = bf16[256,2048]{1,0:T(8,128)(2,1)} fusion(bf16[256,1024]{1,0:T(8,128)(2,1)S(1)} %get-tuple-element.20, bf16[1024,2048]{1,0:T(8,128)(2,1)S(1)} %copy-done.13), kind=kOutput, calls=%fused_computation.5 | convolution fusion | flops 1074266112 | bytes 5767168 | tf_op jit(solution)/shard_map/dot_general | solution.py:297
  89.7 0.0 reduce-scatter.3.cloned.1.call-update
  89.8 0.2 reduce-scatter.5.cloned.1.call-start
  90.0 0.0 all-gather.5.cloned.1.call-done
  90.0 1.9 %convolution_convert_fusion.4 = bf16[256,272]{0,1:T(8,128)(2,1)S(1)} fusion(bf16[256,2048]{1,0:T(8,128)(2,1)} %bitcast.34, bf16[2048,16]{1,0:T(8,128)(2,1)S(1)} %copy.64, bf16[2048,256]{1,0:T(8,128)(2,1)S(1)} %copy-done.15), kind=kOutput, calls=%fused_computation.9 | convolution fusion | flops 287510528 | bytes 2301952 | tf_op jit(solution)/shard_map/dot_general | solution.py:279
  91.9 0.2 copy.68.bcdt_ref
  92.1 6.2 %convolution_convert_fusion.2.zx_ref = bf16[256,2048]{1,0:T(8,128)(2,1)S(1)} fusion(bf16[256,2048]{1,0:T(8,128)(2,1)} %bitcast.35, bf16[2048,2048]{1,0:T(8,128)(2,1)} %bitcast.28), kind=kOutput, calls=%fused_computation.6 | convolution fusion | flops 2148007936 | bytes 10485760 | tf_op jit(solution)/shard_map/dot_general | solution.py:278
  98.3 13.9 %core.3 = (bf16[256,1024]{1,0:T(8,128)(2,1)S(1)}, f32[256,1]{1,0:T(8,128)S(1)}, f32[32,16,64,128]{3,2,1,0:T(8,128)}, f32[32,3,1024]{2,1,0:T(4,128)S(1)}, f32[32,3,256]{2,1,0:T(4,128)S(1)}) custom-call(s32[32]{0:T(128)S(1)} %select_reduce_fusion.counted_ref, ...), custom_call_target="tpu_custom_call", output_to_operand_aliasing={{2}: (10, {}), {3}: (11, {}), {4}: (12, {})} | custom-call | flops 536870912 | bytes 16777216 | tf_op jit(solution)/shard_map/core/pallas_call | solution.py:163
  112.3 2.2 %convolution_convert_fusion = bf16[256,2048]{1,0:T(8,128)(2,1)} fusion(bf16[256,1024]{1,0:T(8,128)(2,1)S(1)} %get-tuple-element.25, bf16[1024,2048]{1,0:T(8,128)(2,1)S(1)} %copy-done.14), kind=kOutput, calls=%fused_computation.4 | convolution fusion | flops 1074266112 | bytes 5767168 | tf_op jit(solution)/shard_map/dot_general | solution.py:297
  114.5 2.1 %reduce-scatter.3.cloned.1.call-done = bf16[256,512]{1,0:T(8,128)(2,1)} async-done(((bf16[256,2048]{1,0:T(8,128)(2,1)}), bf16[256,512]{1,0:T(8,128)(2,1)}) %reduce-scatter.3.cloned.1.call-update) | async-done | bytes 262160 | tf_op jit(solution)/shard_map/reduce_scatter | solution.py:300
  116.6 0.0 reduce-scatter.5.cloned.1.call-update
  116.6 0.1 dynamic_slice.10
  116.7 0.1 copy.71
  116.7 0.1 copy.72
  116.8 11.9 %all_gather.11 = f32[4,4,128]{2,1,0:T(4,128)S(1)} all-gather(f32[1,4,128]{2,1,0:T(4,128)S(1)} %bitcast.30), channel_id=1, replica_groups=mesh['req'=8,'head'=4] {'head'}, dimensions={0}, use_global_device_ids=true | all-gather | bytes 10240 | tf_op jit(solution)/shard_map/all_gather | solution.py:303
  128.8 0.1 rsqrt.12
  128.9 15.8 %reduce-scatter.5.cloned.1.call-done = bf16[256,512]{1,0:T(8,128)(2,1)} async-done(((bf16[256,2048]{1,0:T(8,128)(2,1)}), bf16[256,512]{1,0:T(8,128)(2,1)}) %reduce-scatter.5.cloned.1.call-update) | async-done | bytes 262160 | tf_op jit(solution)/shard_map/reduce_scatter | solution.py:300
  144.7 1.1 pad_maximum_fusion.3
  145.7 0.2 fusion
  145.9 0.6 gather_fusion.2
  146.5 0.9 broadcast_select_fusion
  147.4 3.7 %all-to-all-start.1 = ((bf16[32,16,512]{2,1,0:T(8,128)(2,1)}), bf16[32,16,512]{2,1,0:T(8,128)(2,1)S(1)}, u32[]{:S(2)}, u32[]{:S(2)}) async-start(bf16[32,16,512]{2,1,0:T(8,128)(2,1)} %broadcast_select_fusion), calls=%async_computation.3 | async-start | bytes 1048576 | tf_op jit(solution)/shard_map/all_to_all | solution.py:307
  151.1 0.1 iota_compare_fusion.4
  151.2 0.7 copy.74
  151.8 1.0 copy.73
  152.8 8.0 %all-to-all-done.1 = bf16[32,16,512]{2,1,0:T(8,128)(2,1)S(1)} async-done(((bf16[32,16,512]{2,1,0:T(8,128)(2,1)}), bf16[32,16,512]{2,1,0:T(8,128)(2,1)S(1)}, u32[]{:S(2)}, u32[]{:S(2)}) %all-to-all-start.1) | async-done | bytes 524320 | tf_op jit(solution)/shard_map/all_to_all | solution.py:307
  160.8 0.6 gather_fusion.3
  161.4 1.0 select_select_fusion
  (47 shorter events, 0.2 us)
Async XLA Ops:
  7.2 2.6 %copy-start = (bf16[32,16,512]{2,1,0:T(8,128)(2,1)S(1)}, bf16[32,16,512]{2,1,0:T(8,128)(2,1)}, u32[]{:S(2)}) copy-start(bf16[32,16,512]{2,1,0:T(8,128)(2,1)} %param.19) | copy-start | bytes 1572868
  7.2 48.1 %copy-start.10 = (f32[16]{0:T(128)S(1)}, f32[16]{0:T(128)}, u32[]{:S(2)}) copy-start(f32[16]{0:T(128)} %param.27) | copy-start | bytes 196
  7.2 48.1 %copy-start.11 = (f32[16]{0:T(128)S(1)}, f32[16]{0:T(128)}, u32[]{:S(2)}) copy-start(f32[16]{0:T(128)} %param.26) | copy-start | bytes 196
  7.2 48.1 %copy-start.12 = (f32[16]{0:T(128)S(1)}, f32[16]{0:T(128)}, u32[]{:S(2)}) copy-start(f32[16]{0:T(128)} %param.25) | copy-start | bytes 196
  7.2 48.1 %copy-start.6 = (f32[32,3,256]{2,0,1:T(8,128)S(1)}, f32[32,3,256]{2,0,1:T(8,128)}, u32[]{:S(2)}) copy-start(f32[32,3,256]{2,0,1:T(8,128)} %param.32) | copy-start | bytes 294916
  7.2 48.2 %copy-start.7 = (bf16[2048,16]{0,1:T(8,128)(2,1)S(1)}, bf16[2048,16]{0,1:T(8,128)(2,1)}, u32[]{:S(2)}) copy-start(bf16[2048,16]{0,1:T(8,128)(2,1)} %param.22) | copy-start | bytes 196612
  7.2 48.5 %copy-start.5 = (f32[32,3,1024]{2,0,1:T(8,128)S(1)}, f32[32,3,1024]{2,0,1:T(8,128)}, u32[]{:S(2)}) copy-start(f32[32,3,1024]{2,0,1:T(8,128)} %param.31) | copy-start | bytes 1179652
  11.3 14.9 %all-to-all-start = ((bf16[32,16,512]{2,1,0:T(8,128)(2,1)}), bf16[32,16,512]{2,1,0:T(8,128)(2,1)S(1)}, u32[]{:S(2)}, u32[]{:S(2)}) async-start(bf16[32,16,512]{2,1,0:T(8,128)(2,1)} %broadcast_select_fusion.2), calls=%async_computation | async-start | bytes 1048576 | tf_op jit(solution)/shard_map/all_to_all | solution.py:260
  16.5 38.8 %all-gather.3.cloned.1.call-start = ((), (), s32[]{:S(2)}) async-start(), calls=%async_computation.4 | async-start | bytes 1310720 | tf_op jit(solution)/shard_map/all_gather | solution.py:274
  27.8 62.2 %all-gather.5.cloned.1.call-start = ((), (), s32[]{:S(2)}) async-start(), calls=%async_computation.6 | async-start | bytes 1310720 | tf_op jit(solution)/shard_map/all_gather | solution.py:274
  55.2 61.3 %reduce-scatter.3.cloned.1.call-start = ((), (), s32[]{:S(2)}) async-start(), calls=%async_computation.5 | async-start | bytes 1310720 | tf_op jit(solution)/shard_map/reduce_scatter | solution.py:300
  56.0 10.3 %copy-start.8 = (s32[256]{0:T(256)S(1)}, s32[256]{0:T(256)}, u32[]{:S(2)}) copy-start(s32[256]{0:T(256)} %param.35) | copy-start | bytes 3076
  56.0 10.3 %copy-start.9 = (s32[256]{0:T(256)S(1)}, s32[256]{0:T(256)}, u32[]{:S(2)}) copy-start(s32[256]{0:T(256)} %param.34) | copy-start | bytes 3076
  56.0 10.5 %copy-start.15 = (bf16[2048,256]{1,0:T(8,128)(2,1)S(1)}, bf16[2048,256]{1,0:T(8,128)(2,1)}, u32[]{:S(2)}) copy-start(bf16[2048,256]{1,0:T(8,128)(2,1)} %param.21) | copy-start | bytes 3145732
  56.0 10.5 %copy-start.16 = (bf16[16,16,2048]{2,1,0:T(8,128)(2,1)S(1)}, bf16[16,16,2048]{2,1,0:T(8,128)(2,1)}, u32[]{:S(2)}) copy-start(bf16[16,16,2048]{2,1,0:T(8,128)(2,1)} %all-gather.3.cloned.1.call-done) | copy-start | bytes 3145732
  67.4 6.1 %copy-start.2 = (f32[5,1024]{1,0:T(8,128)S(1)}, f32[5,1024]{1,0:T(8,128)}, u32[]{:S(2)}) copy-start(f32[5,1024]{1,0:T(8,128)} %cxw_ref.3) | copy-start | bytes 61444
  67.4 6.1 %copy-start.3 = (f32[5,256]{1,0:T(8,128)S(1)}, f32[5,256]{1,0:T(8,128)}, u32[]{:S(2)}) copy-start(f32[5,256]{1,0:T(8,128)} %cbw_ref.3) | copy-start | bytes 15364
  67.4 6.1 %copy-start.4 = (f32[1024]{0:T(1024)S(1)}, f32[1024]{0:T(1024)}, u32[]{:S(2)}) copy-start(f32[1024]{0:T(1024)} %param.28) | copy-start | bytes 12292
  73.6 14.0 %copy-start.13 = (bf16[1024,2048]{1,0:T(8,128)(2,1)S(1)}, bf16[1024,2048]{1,0:T(8,128)(2,1)}, u32[]{:S(2)}) copy-start(bf16[1024,2048]{1,0:T(8,128)(2,1)} %param.29) | copy-start | bytes 12582916
  89.8 54.9 %reduce-scatter.5.cloned.1.call-start = ((), (), s32[]{:S(2)}) async-start(), calls=%async_computation.7 | async-start | bytes 1310720 | tf_op jit(solution)/shard_map/reduce_scatter | solution.py:300
  98.3 14.0 %copy-start.14 = (bf16[1024,2048]{1,0:T(8,128)(2,1)S(1)}, bf16[1024,2048]{1,0:T(8,128)(2,1)}, u32[]{:S(2)}) copy-start(bf16[1024,2048]{1,0:T(8,128)(2,1)} %param.29) | copy-start | bytes 12582916
  128.8 33.6 %copy-start.1 = (bf16[32,16,512]{2,1,0:T(8,128)(2,1)S(1)}, bf16[32,16,512]{2,1,0:T(8,128)(2,1)}, u32[]{:S(2)}) copy-start(bf16[32,16,512]{2,1,0:T(8,128)(2,1)} %param.19) | copy-start | bytes 1572868
  147.4 13.4 %all-to-all-start.1 = ((bf16[32,16,512]{2,1,0:T(8,128)(2,1)}), bf16[32,16,512]{2,1,0:T(8,128)(2,1)S(1)}, u32[]{:S(2)}, u32[]{:S(2)}) async-start(bf16[32,16,512]{2,1,0:T(8,128)(2,1)} %broadcast_select_fusion), calls=%async_computation.3 | async-start | bytes 1048576 | tf_op jit(solution)/shard_map/all_to_all | solution.py:307
Sparse Core Ops, SparseCore 0:
  27.9 27.2 all-gather.2
  57.4 27.3 all-gather.4
  89.9 26.6 reduce-scatter.2
  118.8 25.8 reduce-scatter.4

commit v3 on v2

--- a/solution.py
+++ b/solution.py
@@ -207,6 +207,63 @@
     )(counted, zx, bcdt, states, cx, cbc, cxw, cbw, head_params, gain, *done)
 
 
+def exchange_kernel(peers, per_peer, out_order, in_order, src, dst, outgoing, arrived, send_sem, recv_sem):
+    me = lax.axis_index("req")
+    rows = peers * per_peer
+    barrier = pltpu.get_barrier_semaphore()
+    for step in range(1, peers):
+        pl.semaphore_signal(
+            barrier, inc=1, device_id={"req": lax.rem(me + step, peers)}, device_id_type=pl.DeviceIdType.MESH
+        )
+
+    def gather(i, carry):
+        outgoing[i] = src[out_order[i]]
+        return carry
+
+    lax.fori_loop(0, rows, gather, 0)
+    pl.semaphore_wait(barrier, peers - 1)
+    copies = []
+    for step in range(1, peers):
+        peer = lax.rem(me + step, peers)
+        copy = pltpu.make_async_remote_copy(
+            src_ref=outgoing.at[pl.ds(peer * per_peer, per_peer)],
+            dst_ref=arrived.at[pl.ds(me * per_peer, per_peer)],
+            send_sem=send_sem.at[step - 1],
+            recv_sem=recv_sem.at[step - 1],
+            device_id={"req": peer},
+            device_id_type=pl.DeviceIdType.MESH,
+        )
+        copy.start()
+        copies.append(copy)
+    arrived[pl.ds(me * per_peer, per_peer)] = outgoing[pl.ds(me * per_peer, per_peer)]
+    for copy in copies:
+        copy.wait()
+
+    def scatter(i, carry):
+        dst[i] = arrived[in_order[i]]
+        return carry
+
+    lax.fori_loop(0, rows, scatter, 0)
+
+
+def exchange(array, out_order, in_order, peers):
+    per_peer = array.shape[0] // peers
+    return pl.pallas_call(
+        functools.partial(exchange_kernel, peers, per_peer),
+        out_shape=jax.ShapeDtypeStruct(array.shape, array.dtype),
+        in_specs=[pl.BlockSpec(memory_space=pltpu.SMEM)] * 2 + [pl.BlockSpec(memory_space=pltpu.VMEM)],
+        out_specs=pl.BlockSpec(memory_space=pltpu.VMEM),
+        scratch_shapes=[
+            pltpu.VMEM(array.shape, array.dtype),
+            pltpu.VMEM(array.shape, array.dtype),
+            pltpu.SemaphoreType.DMA((peers - 1,)),
+            pltpu.SemaphoreType.DMA((peers - 1,)),
+        ],
+        compiler_params=pltpu.CompilerParams(collective_id=0, has_side_effects=True),
+        name="exchange",
+    )(out_order, in_order, array)
+
+
 def routes(slot, rows, myself, peers):
     per_peer = rows // peers
     blocks = slot.reshape(peers, rows)
@@ -256,9 +313,7 @@
     hit = jnp.arange(slot.shape[0], dtype=jnp.int32)[None, :] == request[:, None]
     my_counted = jnp.sum(jnp.where(hit, counted[None, :], 0), axis=1, dtype=jnp.int32)
 
-    outgoing = jnp.take(hidden, send_order, axis=0)
-    arrived = lax.all_to_all(outgoing, "req", split_axis=0, concat_axis=0, tiled=True)
-    pooled = jnp.take(arrived, to_pool, axis=0)
+    pooled = exchange(hidden, send_order, to_pool, peers)
     chunks = 2
     part = rows // chunks
     flat_zx = w_zx.reshape(width, 2 * chans)
@@ -270,7 +325,7 @@
     for c in range(chunks):
         piece = pooled[c * part : (c + 1) * part]
         if c > 0:
-            gathered[-1], piece = hold((gathered[-1], piece))
+            gathered[-1], piece, flat_zx = hold((gathered[-1], piece, flat_zx))
         gathered.append(lax.all_gather(piece, "head", axis=2, tiled=True))
     done, squares, summed = (), [], []
     for c in range(chunks):
@@ -304,8 +359,7 @@
     meansq = total / (chans * lax.axis_size("head"))
     full = jnp.concatenate(summed, axis=0).astype(f32)
     result = (full * lax.rsqrt(meansq + 1e-05)).astype(bf16).reshape(rows, steps, width_part)
-    back = lax.all_to_all(jnp.take(result, back_order, axis=0), "req", split_axis=0, concat_axis=0, tiled=True)
-    mine = jnp.take(back, home, axis=0)
+    mine = exchange(result, back_order, home, peers)
     my_lengths = lax.dynamic_slice_in_dim(lengths, myself * rows, rows, 0)
     valid = jnp.arange(steps, dtype=jnp.int32)[None, :] < my_lengths[:, None]
     out = jnp.where(valid[..., None], mine, jnp.zeros((), bf16))

time: 169 us -> 163 us (0.964)
  Pallas kernels: 27.9 us -> 51.2 us
  waiting for transfers between devices: 63 us -> 41 us
  starting transfers between devices: 9.18 us -> 0.34 us
    pallas_call x0 -> x2, Pallas kernels: none -> 23.2 us  [exchange(): pl.pallas_call(functools.partial(exchange_kernel, peers, per_peer), out_s...]
    all_to_all x2 -> x0, waiting for transfers between devices: 17.7 us -> none  [the longest x1 9.66 us: per_device(): lax.all_to_all(outgoing, 'req', split_axis=0, concat_axis=0, tiled=True)]
    all_to_all x2 -> x0, starting transfers between devices: 8.84 us -> none  [the longest x1 5.17 us: per_device(): lax.all_to_all(outgoing, 'req', split_axis=0, concat_axis=0, tiled=True)]
    all_gather x2, waiting for transfers between devices: 27.4 us -> 23 us  [per_device(): gathered.append(lax.all_gather(piece, 'head', axis=2, tiled=True))]
    gather x4 -> x0, local copies, waits for them, and re-layouts: 2.32 us -> none  [the longest x1 0.58 us: per_device(): outgoing = jnp.take(hidden, send_order, axis=0)]
    select_n x7 -> x0, other arithmetic: 1.95 us -> none  [the longest x2 0.92 us: per_device(): outgoing = jnp.take(hidden, send_order, axis=0)]
    unnamed x40 -> x38, local copies, waits for them, and re-layouts: 12.6 us -> 12.7 us
  transfers between devices with their start and end apart: 6 -> 4, of which waited for: 5 -> 4; matrix products, arithmetic and copies ran while one was open for 19% -> 21% of each run, Pallas kernels for 17% -> 17%
where the time goes in v3:
time: 163 us; the launch traced here: 162 us
  Pallas kernels  51.2 us (31%)
  waiting for transfers between devices  41 us (25%)
  matrix products  20.4 us (13%)
  local copies, waits for them, and re-layouts  16 us (10%)
  between operations  14.1 us (9%)
  blocking collectives  12 us (7%)
  other arithmetic  7.3 us (4%)
    pallas_call x2, Pallas kernels, core(): pl.pallas_call(functools.partial(core_kernel, group, offset), grid_spec=p...  27.9 us
    pallas_call x2, Pallas kernels, exchange(): pl.pallas_call(functools.partial(exchange_kernel, peers, per_peer), out_s...  23.2 us
    all_gather x2, waiting for transfers between devices, per_device(): gathered.append(lax.all_gather(piece, 'head', axis=2, tiled=True))  23 us
    reduce_scatter x2, waiting for transfers between devices, per_device(): lax.psum_scatter(shares, 'head', scatter_dimension=1, tiled=True)  18 us
    unnamed x38, local copies, waits for them, and re-layouts  12.7 us
    dot_general x2, matrix products, per_device(): zx = jnp.dot(tokens, flat_zx, preferred_element_type=f32).astype(bf16)  12.1 us
    all_gather x1, blocking collectives, per_device(): lax.all_gather(square, 'head', axis=0)  12 us
    dot_general x2, matrix products, per_device(): shares = jnp.dot(g, w_out, preferred_element_type=f32).astype(bf16)  4.45 us
  transfers between devices with their start and end apart: 4, of which 4 were waited for; matrix products, arithmetic and copies ran while one was open for 21% of the time, Pallas kernels for 17%

profile of v3, /device:TPU:0, one launch (start us, length us, event | category | flops | bytes accessed | tf_op | source)
XLA Modules:
  0.0 162.4 jit_solution(17518873127388041877)
XLA Ops:
  7.2 0.0 all-gather.3.cloned.1.call-start
  7.3 0.8 reshape.166
  8.0 0.3 convert_reduce_fusion
  8.4 0.1 broadcast_add_fusion
  8.4 0.1 add.68
  8.5 0.6 select_reduce_fusion.1.out_order
  9.1 1.4 fusion.2
  10.5 12.4 %exchange.2 = bf16[32,16,512]{2,1,0:T(8,128)(2,1)} custom-call(s32[32]{0:T(128)} %select_reduce_fusion.1.out_order, s32[32]{0:T(128)} %get-tuple-element.55.in_order, bf16[32,16,512]{2,1,0:T(8,128)(2,1)} %src.1), custom_call_target="tpu_custom_call" | custom-call | tf_op jit(solution)/shard_map/exchange/pallas_call | solution.py:251
  22.9 1.9 %fusion.7 = (bf16[16,16,512]{2,1,0:T(8,128)(2,1)}, bf16[16,16,512]{2,1,0:T(8,128)(2,1)}) fusion(bf16[32,16,512]{2,1,0:T(8,128)(2,1)} %exchange.2), kind=kLoop, calls=%fused_computation.40 | loop fusion | bytes 1048576 | tf_op jit(solution)/shard_map/slice | solution.py:326
  24.7 0.0 all-gather.3.cloned.1.call-update
  24.8 0.0 all-gather.5.cloned.1.call-start
  24.8 0.0 copy-start.10
  24.8 0.0 copy-start.11
  24.8 0.0 copy-start.12
  24.9 0.0 copy-start.4
  24.9 0.0 copy-start.5
  24.9 0.0 copy-start.3
  24.9 0.0 copy-start.8
  24.9 0.0 copy-start.9
  24.9 0.0 copy-start.15
  24.9 10.3 %copy.75 = bf16[256,8,2,1024]{3,1,2,0:T(8,128)(2,1)} copy(bf16[256,8,2,1024]{3,2,1,0:T(2,128)(2,1)} %bitcast.25) | data formatting | bytes 16777216
  35.2 0.0 copy-done.7
  35.2 19.2 %all-gather.3.cloned.1.call-done = bf16[16,16,2048]{2,1,0:T(8,128)(2,1)} async-done(((bf16[16,16,512]{2,1,0:T(8,128)(2,1)}), bf16[16,16,2048]{2,1,0:T(8,128)(2,1)}) %all-gather.3.cloned.1.call-update) | async-done | bytes 1048592 | tf_op jit(solution)/shard_map/all_gather | solution.py:329
  54.3 0.0 all-gather.5.cloned.1.call-update
  54.4 0.0 reduce-scatter.3.cloned.1.call-start
  54.5 0.1 copy.67.cbc_ref
  54.6 0.3 copy.64
  54.9 0.0 copy-done.3
  54.9 0.3 copy.66.cx_ref
  55.2 0.2 select_reduce_fusion.counted_ref
  55.4 1.9 %convolution_convert_fusion.5 = bf16[256,272]{0,1:T(8,128)(2,1)S(1)} fusion(bf16[256,2048]{1,0:T(8,128)(2,1)} %bitcast.35, bf16[2048,16]{1,0:T(8,128)(2,1)S(1)} %copy.64, bf16[2048,256]{1,0:T(8,128)(2,1)S(1)} %copy-done.15), kind=kOutput, calls=%fused_computation.6 | convolution fusion | flops 287510528 | bytes 2301952 | tf_op jit(solution)/shard_map/dot_general | solution.py:334
  57.3 0.2 copy.65.bcdt_ref
  57.5 0.0 copy-start
  57.5 0.0 copy-start.1
  57.5 0.0 copy-start.2
  57.5 6.1 %convolution_convert_fusion.3.zx_ref = bf16[256,2048]{1,0:T(8,128)(2,1)S(1)} fusion(bf16[256,2048]{1,0:T(8,128)(2,1)} %bitcast.36, bf16[2048,2048]{1,0:T(8,128)(2,1)} %bitcast.26), kind=kOutput, calls=%fused_computation.3 | convolution fusion | flops 2148007936 | bytes 10485760 | tf_op jit(solution)/shard_map/dot_general | solution.py:333
  63.6 0.0 copy-start.13
  63.6 14.0 %core.2 = (bf16[256,1024]{1,0:T(8,128)(2,1)S(1)}, f32[256,1]{1,0:T(8,128)S(1)}, f32[32,16,64,128]{3,2,1,0:T(8,128)}, f32[32,3,1024]{2,1,0:T(4,128)S(1)}, f32[32,3,256]{2,1,0:T(4,128)S(1)}) custom-call(s32[32]{0:T(128)S(1)} %select_reduce_fusion.counted_ref, bf16[256,2048]{1,0:T(8,128)(2,1)S(1)} %convolution_convert_fusion.3.zx_ref, ...), custom_call_target="tpu_custom_call" | custom-call | flops 536870912 | bytes 16777216 | tf_op jit(solution)/shard_map/core/pallas_call | solution.py:163
  77.6 2.2 %convolution_convert_fusion.1 = bf16[256,2048]{1,0:T(8,128)(2,1)} fusion(bf16[256,1024]{1,0:T(8,128)(2,1)S(1)} %get-tuple-element.21, bf16[1024,2048]{1,0:T(8,128)(2,1)S(1)} %copy-done.13), kind=kOutput, calls=%fused_computation.1 | convolution fusion | flops 1074266112 | bytes 5767168 | tf_op jit(solution)/shard_map/dot_general | solution.py:352
  79.9 0.0 reduce-scatter.3.cloned.1.call-update
  79.9 0.2 reduce-scatter.5.cloned.1.call-start
  80.1 3.8 %all-gather.5.cloned.1.call-done = bf16[16,16,2048]{2,1,0:T(8,128)(2,1)} async-done(((bf16[16,16,512]{2,1,0:T(8,128)(2,1)}), bf16[16,16,2048]{2,1,0:T(8,128)(2,1)}) %all-gather.5.cloned.1.call-update) | async-done | bytes 1048592 | tf_op jit(solution)/shard_map/all_gather | solution.py:329
  83.9 1.9 %convolution_convert_fusion.4 = bf16[256,272]{0,1:T(8,128)(2,1)S(1)} fusion(bf16[256,2048]{1,0:T(8,128)(2,1)} %bitcast.33, bf16[2048,16]{1,0:T(8,128)(2,1)S(1)} %copy.64, bf16[2048,256]{1,0:T(8,128)(2,1)S(1)} %copy-done.15), kind=kOutput, calls=%fused_computation.5 | convolution fusion | flops 287510528 | bytes 2301952 | tf_op jit(solution)/shard_map/dot_general | solution.py:334
  85.9 0.2 copy.68.bcdt_ref
  86.0 6.0 %convolution_convert_fusion.2.zx_ref = bf16[256,2048]{1,0:T(8,128)(2,1)S(1)} fusion(bf16[256,2048]{1,0:T(8,128)(2,1)} %bitcast.34, bf16[2048,2048]{1,0:T(8,128)(2,1)} %bitcast.27), kind=kOutput, calls=%fused_computation.2 | convolution fusion | flops 2148007936 | bytes 10485760 | tf_op jit(solution)/shard_map/dot_general | solution.py:333
  92.1 0.0 copy-start.14
  92.1 13.9 %core.3 = (bf16[256,1024]{1,0:T(8,128)(2,1)S(1)}, f32[256,1]{1,0:T(8,128)S(1)}, f32[32,16,64,128]{3,2,1,0:T(8,128)}, f32[32,3,1024]{2,1,0:T(4,128)S(1)}, f32[32,3,256]{2,1,0:T(4,128)S(1)}) custom-call(s32[32]{0:T(128)S(1)} %select_reduce_fusion.counted_ref, ...), custom_call_target="tpu_custom_call", output_to_operand_aliasing={{2}: (10, {}), {3}: (11, {}), {4}: (12, {})} | custom-call | flops 536870912 | bytes 16777216 | tf_op jit(solution)/shard_map/core/pallas_call | solution.py:163
  106.1 2.2 %convolution_convert_fusion = bf16[256,2048]{1,0:T(8,128)(2,1)} fusion(bf16[256,1024]{1,0:T(8,128)(2,1)S(1)} %get-tuple-element.26, bf16[1024,2048]{1,0:T(8,128)(2,1)S(1)} %copy-done.14), kind=kOutput, calls=%fused_computation | convolution fusion | flops 1074266112 | bytes 5767168 | tf_op jit(solution)/shard_map/dot_general | solution.py:352
  108.3 4.6 %reduce-scatter.3.cloned.1.call-done = bf16[256,512]{1,0:T(8,128)(2,1)} async-done(((bf16[256,2048]{1,0:T(8,128)(2,1)}), bf16[256,512]{1,0:T(8,128)(2,1)}) %reduce-scatter.3.cloned.1.call-update) | async-done | bytes 262160 | tf_op jit(solution)/shard_map/reduce_scatter | solution.py:355
  112.9 0.0 reduce-scatter.5.cloned.1.call-update
  112.9 0.1 dynamic_slice.10
  113.0 0.6 select_reduce_fusion.2.out_order
  113.6 0.1 iota_compare_fusion.4
  113.7 0.1 copy.71
  113.8 0.1 copy.72
  113.9 12.0 %all_gather.11 = f32[4,4,128]{2,1,0:T(4,128)S(1)} all-gather(f32[1,4,128]{2,1,0:T(4,128)S(1)} %bitcast.29), channel_id=1, replica_groups=mesh['req'=8,'head'=4] {'head'}, dimensions={0}, use_global_device_ids=true | all-gather | bytes 10240 | tf_op jit(solution)/shard_map/all_gather | solution.py:358
  125.9 0.1 rsqrt.12
  126.0 0.7 copy.74
  126.7 1.0 copy.73
  127.6 13.4 %reduce-scatter.5.cloned.1.call-done = bf16[256,512]{1,0:T(8,128)(2,1)} async-done(((bf16[256,2048]{1,0:T(8,128)(2,1)}), bf16[256,512]{1,0:T(8,128)(2,1)}) %reduce-scatter.5.cloned.1.call-update) | async-done | bytes 262160 | tf_op jit(solution)/shard_map/reduce_scatter | solution.py:355
  141.0 1.1 pad_maximum_fusion.3
  142.1 1.0 fusion.src
  143.0 10.9 %exchange.3 = bf16[32,16,512]{2,1,0:T(8,128)(2,1)} custom-call(s32[32]{0:T(128)} %select_reduce_fusion.2.out_order, s32[32]{0:T(128)} %copy-done.7, bf16[32,16,512]{2,1,0:T(8,128)(2,1)} %fusion.src), custom_call_target="tpu_custom_call" | custom-call | tf_op jit(solution)/shard_map/exchange/pallas_call | solution.py:251
  153.9 2.0 %broadcast_select_fusion = bf16[32,16,512]{2,1,0:T(8,128)(2,1)} fusion(bf16[32,16,512]{2,1,0:T(8,128)(2,1)} %exchange.3, pred[32,16]{1,0:T(8,128)(4,1)S(1)} %iota_compare_fusion.4), kind=kLoop, calls=%fused_computation.10 | loop fusion | flops 262144 | bytes 1049088 | tf_op jit(solution)/shard_map/jit(_where)/select_n | solution.py:365
  (26 shorter events, 0.1 us)
Async XLA Ops:
  7.2 47.2 %all-gather.3.cloned.1.call-start = ((), (), s32[]{:S(2)}) async-start(), calls=%async_computation.2 | async-start | bytes 1310720 | tf_op jit(solution)/shard_map/all_gather | solution.py:329
  8.3 26.8 %copy-start.7 = (s32[32]{0:T(128)}, s32[32]{0:T(128)S(1)}, u32[]{:S(2)}) copy-start(s32[32]{0:T(128)S(1)} %add_bitcast_fusion.in_order) | copy-start | bytes 388
  24.8 59.2 %all-gather.5.cloned.1.call-start = ((), (), s32[]{:S(2)}) async-start(), calls=%async_computation.4 | async-start | bytes 1310720 | tf_op jit(solution)/shard_map/all_gather | solution.py:329
  24.8 29.6 %copy-start.10 = (f32[16]{0:T(128)S(1)}, f32[16]{0:T(128)}, u32[]{:S(2)}) copy-start(f32[16]{0:T(128)} %param.25) | copy-start | bytes 196
  24.8 29.6 %copy-start.11 = (f32[16]{0:T(128)S(1)}, f32[16]{0:T(128)}, u32[]{:S(2)}) copy-start(f32[16]{0:T(128)} %param.24) | copy-start | bytes 196
  24.8 29.6 %copy-start.12 = (f32[16]{0:T(128)S(1)}, f32[16]{0:T(128)}, u32[]{:S(2)}) copy-start(f32[16]{0:T(128)} %param.23) | copy-start | bytes 196
  24.9 29.6 %copy-start.4 = (f32[32,3,256]{2,0,1:T(8,128)S(1)}, f32[32,3,256]{2,0,1:T(8,128)}, u32[]{:S(2)}) copy-start(f32[32,3,256]{2,0,1:T(8,128)} %param.30) | copy-start | bytes 294916
  24.9 29.7 %copy-start.5 = (bf16[2048,16]{0,1:T(8,128)(2,1)S(1)}, bf16[2048,16]{0,1:T(8,128)(2,1)}, u32[]{:S(2)}) copy-start(bf16[2048,16]{0,1:T(8,128)(2,1)} %param.20) | copy-start | bytes 196612
  24.9 30.0 %copy-start.3 = (f32[32,3,1024]{2,0,1:T(8,128)S(1)}, f32[32,3,1024]{2,0,1:T(8,128)}, u32[]{:S(2)}) copy-start(f32[32,3,1024]{2,0,1:T(8,128)} %param.29) | copy-start | bytes 1179652
  24.9 30.3 %copy-start.8 = (s32[256]{0:T(256)S(1)}, s32[256]{0:T(256)}, u32[]{:S(2)}) copy-start(s32[256]{0:T(256)} %param.33) | copy-start | bytes 3076
  24.9 30.3 %copy-start.9 = (s32[256]{0:T(256)S(1)}, s32[256]{0:T(256)}, u32[]{:S(2)}) copy-start(s32[256]{0:T(256)} %param.32) | copy-start | bytes 3076
  24.9 30.5 %copy-start.15 = (bf16[2048,256]{1,0:T(8,128)(2,1)S(1)}, bf16[2048,256]{1,0:T(8,128)(2,1)}, u32[]{:S(2)}) copy-start(bf16[2048,256]{1,0:T(8,128)(2,1)} %param.19) | copy-start | bytes 3145732
  54.4 58.5 %reduce-scatter.3.cloned.1.call-start = ((), (), s32[]{:S(2)}) async-start(), calls=%async_computation.3 | async-start | bytes 1310720 | tf_op jit(solution)/shard_map/reduce_scatter | solution.py:355
  57.5 6.1 %copy-start = (f32[5,1024]{1,0:T(8,128)S(1)}, f32[5,1024]{1,0:T(8,128)}, u32[]{:S(2)}) copy-start(f32[5,1024]{1,0:T(8,128)} %cxw_ref.3) | copy-start | bytes 61444
  57.5 6.1 %copy-start.1 = (f32[5,256]{1,0:T(8,128)S(1)}, f32[5,256]{1,0:T(8,128)}, u32[]{:S(2)}) copy-start(f32[5,256]{1,0:T(8,128)} %cbw_ref.3) | copy-start | bytes 15364
  57.5 6.1 %copy-start.2 = (f32[1024]{0:T(1024)S(1)}, f32[1024]{0:T(1024)}, u32[]{:S(2)}) copy-start(f32[1024]{0:T(1024)} %param.26) | copy-start | bytes 12292
  63.6 14.0 %copy-start.13 = (bf16[1024,2048]{1,0:T(8,128)(2,1)S(1)}, bf16[1024,2048]{1,0:T(8,128)(2,1)}, u32[]{:S(2)}) copy-start(bf16[1024,2048]{1,0:T(8,128)(2,1)} %param.27) | copy-start | bytes 12582916
  79.9 61.1 %reduce-scatter.5.cloned.1.call-start = ((), (), s32[]{:S(2)}) async-start(), calls=%async_computation.5 | async-start | bytes 1310720 | tf_op jit(solution)/shard_map/reduce_scatter | solution.py:355
  92.1 14.0 %copy-start.14 = (bf16[1024,2048]{1,0:T(8,128)(2,1)S(1)}, bf16[1024,2048]{1,0:T(8,128)(2,1)}, u32[]{:S(2)}) copy-start(bf16[1024,2048]{1,0:T(8,128)(2,1)} %param.27) | copy-start | bytes 12582916
  106.1 7.0 %copy-start.6 = (s32[32]{0:T(128)S(1)}, s32[32]{0:T(128)}, u32[]{:S(2)}) copy-start(s32[32]{0:T(128)} %get-tuple-element.55.in_order) | copy-start | bytes 388
Sparse Core Ops, SparseCore 0:
  24.9 29.4 all-gather.2
  56.5 27.4 all-gather.4
  86.2 26.6 reduce-scatter.2
  115.2 25.7 reduce-scatter.4

commit v4 on v3

--- a/solution.py
+++ b/solution.py
@@ -264,6 +264,13 @@
     )(out_order, in_order, array)
 
 
+def gather_head(piece):
+    n = lax.axis_size("head")
+    me = lax.axis_index("head")
+    parts = [piece] + [lax.ppermute(piece, "head", [(i, (i + d) % n) for i in range(n)]) for d in range(1, n)]
+    return jnp.concatenate([lax.select_n(lax.rem(me - j + n, n), *parts) for j in range(n)], axis=2)
+
+
 def routes(slot, rows, myself, peers):
     per_peer = rows // peers
     blocks = slot.reshape(peers, rows)
@@ -326,7 +333,7 @@
         piece = pooled[c * part : (c + 1) * part]
         if c > 0:
             gathered[-1], piece, flat_zx = hold((gathered[-1], piece, flat_zx))
-        gathered.append(lax.all_gather(piece, "head", axis=2, tiled=True))
+        gathered.append(gather_head(piece))
     done, squares, summed = (), [], []
     for c in range(chunks):
         tokens = gathered[c].reshape(part * steps, width)

time: 163 us -> 157 us (0.963)
  waiting for transfers between devices: 41 us -> 18.9 us
  starting transfers between devices: 0.34 us -> 14.1 us
  other arithmetic: 7.3 us -> 10.1 us
  matrix products: 20.4 us -> 18.4 us
    all_gather x2 -> x0, waiting for transfers between devices: 23 us -> none  [per_device(): gathered.append(lax.all_gather(piece, 'head', axis=2, tiled=True))]
    ppermute x0 -> x6, starting transfers between devices: none -> 13.8 us  [gather_head(): lax.ppermute(piece, 'head', [(i, (i + d) % n) for i in range(n)])]
    ppermute x0 -> x6, waiting for transfers between devices: none -> 5.14 us  [gather_head(): lax.ppermute(piece, 'head', [(i, (i + d) % n) for i in range(n)])]
    reduce_scatter x2, waiting for transfers between devices: 18 us -> 13.7 us  [per_device(): lax.psum_scatter(shares, 'head', scatter_dimension=1, tiled=True)]
    select_n x0 -> x2, other arithmetic: none -> 2.54 us  [gather_head(): lax.select_n(lax.rem(me - j + n, n), *parts)]
    dot_general x2, matrix products: 3.85 us -> 2.05 us  [per_device(): bcdt = jnp.dot(tokens, w_bcdt, preferred_element_type=f32).astype(bf16)]
    unnamed x38 -> x48, local copies, waits for them, and re-layouts: 12.7 us -> 14 us
  transfers between devices with their start and end apart: 4 -> 8, of which waited for: 4 -> 3; matrix products, arithmetic and copies ran while one was open for 21% -> 22% of each run, Pallas kernels for 17% -> 18%
where the time goes in v4:
time: 157 us
  Pallas kernels  51.2 us (33%)
  waiting for transfers between devices  18.9 us (12%)
  matrix products  18.4 us (12%)
  local copies, waits for them, and re-layouts  17.5 us (11%)
  between operations  14.5 us (9%)
  starting transfers between devices  14.1 us (9%)
  blocking collectives  12 us (8%)
  other arithmetic  10.1 us (6%)
    pallas_call x2, Pallas kernels, core(): pl.pallas_call(functools.partial(core_kernel, group, offset), grid_spec=p...  27.9 us
    pallas_call x2, Pallas kernels, exchange(): pl.pallas_call(functools.partial(exchange_kernel, peers, per_peer), out_s...  23.3 us
    unnamed x48, local copies, waits for them, and re-layouts  14 us
    ppermute x6, starting transfers between devices, gather_head(): lax.ppermute(piece, 'head', [(i, (i + d) % n) for i in range(n)])  13.8 us
    reduce_scatter x2, waiting for transfers between devices, per_device(): lax.psum_scatter(shares, 'head', scatter_dimension=1, tiled=True)  13.7 us
    all_gather x1, blocking collectives, per_device(): lax.all_gather(square, 'head', axis=0)  12 us
    dot_general x2, matrix products, per_device(): zx = jnp.dot(tokens, flat_zx, preferred_element_type=f32).astype(bf16)  11.8 us
    ppermute x6, waiting for transfers between devices, gather_head(): lax.ppermute(piece, 'head', [(i, (i + d) % n) for i in range(n)])  5.14 us
  transfers between devices with their start and end apart: 8, of which 3 were waited for; matrix products, arithmetic and copies ran while one was open for 22% of the time, Pallas kernels for 18%

profile of v4, /device:TPU:0, one launch (start us, length us, event | category | flops | bytes accessed | tf_op | source)
XLA Modules:
  0.0 156.7 jit_solution(14187465174686235900)
XLA Ops:
  7.2 0.0 reduce-scatter.3.cloned.1.call-start
  7.3 0.8 reshape.166
  8.1 0.3 convert_reduce_fusion
  8.5 0.1 broadcast_add_fusion
  8.5 0.1 add.93
  8.6 0.6 select_reduce_fusion.1.out_order
  9.2 1.4 fusion.2
  10.6 12.4 %exchange.2 = bf16[32,16,512]{2,1,0:T(8,128)(2,1)} custom-call(s32[32]{0:T(128)} %select_reduce_fusion.1.out_order, s32[32]{0:T(128)} %get-tuple-element.55.in_order, bf16[32,16,512]{2,1,0:T(8,128)(2,1)} %src.1), custom_call_target="tpu_custom_call" | custom-call | tf_op jit(solution)/shard_map/exchange/pallas_call | solution.py:251
  23.0 1.1 fusion.7
  24.1 2.7 %collective-permute-start.1 = (bf16[16,16,512]{2,1,0:T(8,128)(2,1)S(1)}, bf16[16,16,512]{2,1,0:T(8,128)(2,1)S(1)}, u32[]{:S(2)}, u32[]{:S(2)}) collective-permute-start(bf16[16,16,512]{2,1,0:T(8,128)(2,1)S(1)} %get-tuple-element.65), channel_id=1, source_target_pairs={{0,2},{1,3},{2,0},{3,1},{4,6},{5,7},{6,4},{7,5},{8,10},{9,11},{10,... | collective-permute-start | bytes 786440 | tf_op jit(solution)/shard_map/ppermute | solution.py:270
  26.8 1.3 collective-permute-start.2
  28.1 0.7 collective-permute-start
  28.8 0.1 copy.67.cbc_ref
  28.9 0.3 copy.64
  29.2 0.3 copy.66.cx_ref
  29.5 0.0 copy-start.12
  29.5 0.0 copy-start.13
  29.5 0.0 copy-start.14
  29.5 0.0 copy-start.15
  29.5 0.0 copy-start.16
  29.5 10.2 %copy.75 = bf16[256,8,2,1024]{3,1,2,0:T(8,128)(2,1)} copy(bf16[256,8,2,1024]{3,2,1,0:T(2,128)(2,1)} %bitcast.25) | data formatting | bytes 16777216
  39.8 0.2 select_reduce_fusion.counted_ref
  40.0 0.0 copy-start.5
  40.0 0.7 copy-done.5
  40.7 0.7 copy-done.6
  41.4 5.1 %collective-permute-done = bf16[16,16,512]{2,1,0:T(8,128)(2,1)} collective-permute-done((bf16[16,16,512]{2,1,0:T(8,128)(2,1)S(1)}, bf16[16,16,512]{2,1,0:T(8,128)(2,1)}, u32[]{:S(2)}, u32[]{:S(2)}) %collective-permute-start) | collective-permute-done | bytes 262176 | tf_op jit(solution)/shard_map/ppermute | solution.py:270
  46.5 1.2 select_select_fusion.7
  47.8 0.1 pad_maximum_fusion.1
  47.9 3.8 %collective-permute-start.5 = (bf16[16,16,512]{2,1,0:T(8,128)(2,1)S(1)}, bf16[16,16,512]{2,1,0:T(8,128)(2,1)}, u32[]{:S(2)}, u32[]{:S(2)}) collective-permute-start(bf16[16,16,512]{2,1,0:T(8,128)(2,1)S(1)} %get-tuple-element.22), channel_id=1, source_target_pairs={{0,3},{1,0},{2,1},{3,2},{4,7},{5,4},{6,5},{7,6},{8,11},{9,8},{10,9... | collective-permute-start | bytes 786440 | tf_op jit(solution)/shard_map/ppermute | solution.py:270
  51.7 3.4 %collective-permute-start.4 = (bf16[16,16,512]{2,1,0:T(8,128)(2,1)S(1)}, bf16[16,16,512]{2,1,0:T(8,128)(2,1)}, u32[]{:S(2)}, u32[]{:S(2)}) collective-permute-start(bf16[16,16,512]{2,1,0:T(8,128)(2,1)S(1)} %get-tuple-element.22), channel_id=1, source_target_pairs={{0,2},{1,3},{2,0},{3,1},{4,6},{5,7},{6,4},{7,5},{8,10},{9,11},{10,... | collective-permute-start | bytes 786440 | tf_op jit(solution)/shard_map/ppermute | solution.py:270
  55.1 1.9 %collective-permute-start.3 = (bf16[16,16,512]{2,1,0:T(8,128)(2,1)S(1)}, bf16[16,16,512]{2,1,0:T(8,128)(2,1)}, u32[]{:S(2)}, u32[]{:S(2)}) collective-permute-start(bf16[16,16,512]{2,1,0:T(8,128)(2,1)S(1)} %get-tuple-element.22), channel_id=1, source_target_pairs={{0,1},{1,2},{2,3},{3,0},{4,5},{5,6},{6,7},{7,4},{8,9},{9,10},{10,1... | collective-permute-start | bytes 786440 | tf_op jit(solution)/shard_map/ppermute | solution.py:270
  57.0 5.8 %convolution_convert_fusion.3.zx_ref = bf16[256,2048]{1,0:T(8,128)(2,1)S(1)} fusion(bf16[256,2048]{1,0:T(8,128)(2,1)S(1)} %bitcast.29, bf16[2048,2048]{1,0:T(8,128)(2,1)} %bitcast.26), kind=kOutput, calls=%fused_computation.3 | convolution fusion | flops 2148007936 | bytes 10485760 | tf_op jit(solution)/shard_map/dot_general | solution.py:340
  62.9 0.0 copy-start
  62.9 0.0 copy-start.1
  62.9 0.7 convolution_convert_fusion.5
  63.6 0.2 copy.65.bcdt_ref
  63.8 0.0 copy-start.17
  63.8 13.9 %core.2 = (bf16[256,1024]{1,0:T(8,128)(2,1)S(1)}, f32[256,1]{1,0:T(8,128)S(1)}, f32[32,16,64,128]{3,2,1,0:T(8,128)}, f32[32,3,1024]{2,1,0:T(4,128)S(1)}, f32[32,3,256]{2,1,0:T(4,128)S(1)}) custom-call(s32[32]{0:T(128)S(1)} %select_reduce_fusion.counted_ref, bf16[256,2048]{1,0:T(8,128)(2,1)S(1)} %convolution_convert_fusion.3.zx_ref, ...), custom_call_target="tpu_custom_call" | custom-call | flops 536870912 | bytes 16777216 | tf_op jit(solution)/shard_map/core/pallas_call | solution.py:163
  77.8 2.3 %convolution_convert_fusion.1 = bf16[256,2048]{1,0:T(8,128)(2,1)} fusion(bf16[256,1024]{1,0:T(8,128)(2,1)S(1)} %get-tuple-element.21, bf16[1024,2048]{1,0:T(8,128)(2,1)S(1)} %copy-done.17), kind=kOutput, calls=%fused_computation.1 | convolution fusion | flops 1074266112 | bytes 5767168 | tf_op jit(solution)/shard_map/dot_general | solution.py:359
  80.1 0.0 reduce-scatter.3.cloned.1.call-update
  80.1 0.2 reduce-scatter.5.cloned.1.call-start
  80.4 1.3 select_select_fusion.3
  81.7 0.1 pad_maximum_fusion.2
  81.8 1.4 convolution_convert_fusion.4
  83.2 1.1 copy.68.bcdt_ref
  84.3 5.9 %convolution_convert_fusion.2.zx_ref = bf16[256,2048]{1,0:T(8,128)(2,1)S(1)} fusion(bf16[256,2048]{1,0:T(8,128)(2,1)S(1)} %bitcast.32, bf16[2048,2048]{1,0:T(8,128)(2,1)} %bitcast.27), kind=kOutput, calls=%fused_computation.2 | convolution fusion | flops 2148007936 | bytes 10485760 | tf_op jit(solution)/shard_map/dot_general | solution.py:340
  90.2 14.0 %core.3 = (bf16[256,1024]{1,0:T(8,128)(2,1)S(1)}, f32[256,1]{1,0:T(8,128)S(1)}, f32[32,16,64,128]{3,2,1,0:T(8,128)}, f32[32,3,1024]{2,1,0:T(4,128)S(1)}, f32[32,3,256]{2,1,0:T(4,128)S(1)}) custom-call(s32[32]{0:T(128)S(1)} %select_reduce_fusion.counted_ref, ...), custom_call_target="tpu_custom_call", output_to_operand_aliasing={{2}: (10, {}), {3}: (11, {}), {4}: (12, {})} | custom-call | flops 536870912 | bytes 16777216 | tf_op jit(solution)/shard_map/core/pallas_call | solution.py:163
  104.2 2.2 %convolution_convert_fusion = bf16[256,2048]{1,0:T(8,128)(2,1)} fusion(bf16[256,1024]{1,0:T(8,128)(2,1)S(1)} %get-tuple-element.26, bf16[1024,2048]{1,0:T(8,128)(2,1)S(1)} %copy-done.18), kind=kOutput, calls=%fused_computation | convolution fusion | flops 1074266112 | bytes 5767168 | tf_op jit(solution)/shard_map/dot_general | solution.py:359
  106.4 0.3 reduce-scatter.3.cloned.1.call-done
  106.8 0.0 reduce-scatter.5.cloned.1.call-update
  106.8 0.1 dynamic_slice.10
  106.9 0.7 select_reduce_fusion.2.out_order
  107.6 0.1 iota_compare_fusion.4
  107.6 0.1 copy.71
  107.7 0.1 copy.72
  107.8 12.0 %all_gather.3 = f32[4,4,128]{2,1,0:T(4,128)S(1)} all-gather(f32[1,4,128]{2,1,0:T(4,128)S(1)} %bitcast.33), channel_id=1, replica_groups=mesh['req'=8,'head'=4] {'head'}, dimensions={0}, use_global_device_ids=true | all-gather | bytes 10240 | tf_op jit(solution)/shard_map/all_gather | solution.py:365
  119.9 0.1 rsqrt.12
  120.0 0.7 copy.74
  120.6 1.0 copy.73
  121.6 13.4 %reduce-scatter.5.cloned.1.call-done = bf16[256,512]{1,0:T(8,128)(2,1)} async-done(((bf16[256,2048]{1,0:T(8,128)(2,1)}), bf16[256,512]{1,0:T(8,128)(2,1)}) %reduce-scatter.5.cloned.1.call-update) | async-done | bytes 262160 | tf_op jit(solution)/shard_map/reduce_scatter | solution.py:362
  135.0 1.0 pad_maximum_fusion.5
  136.0 1.0 fusion.src
  137.0 10.9 %exchange.3 = bf16[32,16,512]{2,1,0:T(8,128)(2,1)} custom-call(s32[32]{0:T(128)} %select_reduce_fusion.2.out_order, s32[32]{0:T(128)} %copy-done.11, bf16[32,16,512]{2,1,0:T(8,128)(2,1)} %fusion.src), custom_call_target="tpu_custom_call" | custom-call | tf_op jit(solution)/shard_map/exchange/pallas_call | solution.py:251
  147.8 2.0 %broadcast_select_fusion = bf16[32,16,512]{2,1,0:T(8,128)(2,1)} fusion(bf16[32,16,512]{2,1,0:T(8,128)(2,1)} %exchange.3, pred[32,16]{1,0:T(8,128)(4,1)S(1)} %iota_compare_fusion.4), kind=kLoop, calls=%fused_computation.12 | loop fusion | flops 262144 | bytes 1049088 | tf_op jit(solution)/shard_map/jit(_where)/select_n | solution.py:372
  (46 shorter events, 0.2 us)
Async XLA Ops:
  7.2 21.6 %copy-start.8 = (f32[32,3,256]{2,0,1:T(8,128)S(1)}, f32[32,3,256]{2,0,1:T(8,128)}, u32[]{:S(2)}) copy-start(f32[32,3,256]{2,0,1:T(8,128)} %param.30) | copy-start | bytes 294916
  7.2 21.7 %copy-start.9 = (bf16[2048,16]{0,1:T(8,128)(2,1)S(1)}, bf16[2048,16]{0,1:T(8,128)(2,1)}, u32[]{:S(2)}) copy-start(bf16[2048,16]{0,1:T(8,128)(2,1)} %param.20) | copy-start | bytes 196612
  7.2 22.0 %copy-start.4 = (f32[32,3,1024]{2,0,1:T(8,128)S(1)}, f32[32,3,1024]{2,0,1:T(8,128)}, u32[]{:S(2)}) copy-start(f32[32,3,1024]{2,0,1:T(8,128)} %param.29) | copy-start | bytes 1179652
  7.2 99.6 %reduce-scatter.3.cloned.1.call-start = ((), (), s32[]{:S(2)}) async-start(), calls=%async_computation.2 | async-start | bytes 1310720 | tf_op jit(solution)/shard_map/reduce_scatter | solution.py:362
  8.4 31.3 %copy-start.11 = (s32[32]{0:T(128)}, s32[32]{0:T(128)S(1)}, u32[]{:S(2)}) copy-start(s32[32]{0:T(128)S(1)} %add_bitcast_fusion.in_order) | copy-start | bytes 388
  24.1 15.9 %collective-permute-start.1 = (bf16[16,16,512]{2,1,0:T(8,128)(2,1)S(1)}, bf16[16,16,512]{2,1,0:T(8,128)(2,1)S(1)}, u32[]{:S(2)}, u32[]{:S(2)}) collective-permute-start(bf16[16,16,512]{2,1,0:T(8,128)(2,1)S(1)} %get-tuple-element.65), channel_id=1, source_target_pairs={{0,2},{1,3},{2,0},{3,1},{4,6},{5,7},{6,4},{7,5},{8,10},{9,11},{10,... | collective-permute-start | bytes 786440 | tf_op jit(solution)/shard_map/ppermute | solution.py:270
  26.8 13.3 %collective-permute-start.2 = (bf16[16,16,512]{2,1,0:T(8,128)(2,1)S(1)}, bf16[16,16,512]{2,1,0:T(8,128)(2,1)S(1)}, u32[]{:S(2)}, u32[]{:S(2)}) collective-permute-start(bf16[16,16,512]{2,1,0:T(8,128)(2,1)S(1)} %get-tuple-element.65), channel_id=1, source_target_pairs={{0,3},{1,0},{2,1},{3,2},{4,7},{5,4},{6,5},{7,6},{8,11},{9,8},{10,9... | collective-permute-start | bytes 786440 | tf_op jit(solution)/shard_map/ppermute | solution.py:270
  28.1 18.4 %collective-permute-start = (bf16[16,16,512]{2,1,0:T(8,128)(2,1)S(1)}, bf16[16,16,512]{2,1,0:T(8,128)(2,1)}, u32[]{:S(2)}, u32[]{:S(2)}) collective-permute-start(bf16[16,16,512]{2,1,0:T(8,128)(2,1)S(1)} %get-tuple-element.65), channel_id=1, source_target_pairs={{0,1},{1,2},{2,3},{3,0},{4,5},{5,6},{6,7},{7,4},{8,9},{9,10},{10,1... | collective-permute-start | bytes 786440 | tf_op jit(solution)/shard_map/ppermute | solution.py:270
  29.5 10.3 %copy-start.12 = (s32[256]{0:T(256)S(1)}, s32[256]{0:T(256)}, u32[]{:S(2)}) copy-start(s32[256]{0:T(256)} %param.33) | copy-start | bytes 3076
  29.5 10.3 %copy-start.13 = (s32[256]{0:T(256)S(1)}, s32[256]{0:T(256)}, u32[]{:S(2)}) copy-start(s32[256]{0:T(256)} %param.32) | copy-start | bytes 3076
  29.5 10.3 %copy-start.14 = (f32[16]{0:T(128)S(1)}, f32[16]{0:T(128)}, u32[]{:S(2)}) copy-start(f32[16]{0:T(128)} %param.25) | copy-start | bytes 196
  29.5 10.3 %copy-start.15 = (f32[16]{0:T(128)S(1)}, f32[16]{0:T(128)}, u32[]{:S(2)}) copy-start(f32[16]{0:T(128)} %param.24) | copy-start | bytes 196
  29.5 10.3 %copy-start.16 = (f32[16]{0:T(128)S(1)}, f32[16]{0:T(128)}, u32[]{:S(2)}) copy-start(f32[16]{0:T(128)} %param.23) | copy-start | bytes 196
  29.5 17.0 %copy-start.3 = (bf16[32,16,512]{2,1,0:T(8,128)(2,1)S(1)}, bf16[32,16,512]{2,1,0:T(8,128)(2,1)}, u32[]{:S(2)}) copy-start(bf16[32,16,512]{2,1,0:T(8,128)(2,1)} %exchange.2) | copy-start | bytes 1572868
  40.0 0.7 copy-start.5
  40.7 0.7 copy-start.6
  47.9 32.5 %collective-permute-start.5 = (bf16[16,16,512]{2,1,0:T(8,128)(2,1)S(1)}, bf16[16,16,512]{2,1,0:T(8,128)(2,1)}, u32[]{:S(2)}, u32[]{:S(2)}) collective-permute-start(bf16[16,16,512]{2,1,0:T(8,128)(2,1)S(1)} %get-tuple-element.22), channel_id=1, source_target_pairs={{0,3},{1,0},{2,1},{3,2},{4,7},{5,4},{6,5},{7,6},{8,11},{9,8},{10,9... | collective-permute-start | bytes 786440 | tf_op jit(solution)/shard_map/ppermute | solution.py:270
  51.7 28.7 %collective-permute-start.4 = (bf16[16,16,512]{2,1,0:T(8,128)(2,1)S(1)}, bf16[16,16,512]{2,1,0:T(8,128)(2,1)}, u32[]{:S(2)}, u32[]{:S(2)}) collective-permute-start(bf16[16,16,512]{2,1,0:T(8,128)(2,1)S(1)} %get-tuple-element.22), channel_id=1, source_target_pairs={{0,2},{1,3},{2,0},{3,1},{4,6},{5,7},{6,4},{7,5},{8,10},{9,11},{10,... | collective-permute-start | bytes 786440 | tf_op jit(solution)/shard_map/ppermute | solution.py:270
  55.1 25.3 %collective-permute-start.3 = (bf16[16,16,512]{2,1,0:T(8,128)(2,1)S(1)}, bf16[16,16,512]{2,1,0:T(8,128)(2,1)}, u32[]{:S(2)}, u32[]{:S(2)}) collective-permute-start(bf16[16,16,512]{2,1,0:T(8,128)(2,1)S(1)} %get-tuple-element.22), channel_id=1, source_target_pairs={{0,1},{1,2},{2,3},{3,0},{4,5},{5,6},{6,7},{7,4},{8,9},{9,10},{10,1... | collective-permute-start | bytes 786440 | tf_op jit(solution)/shard_map/ppermute | solution.py:270
  57.0 5.8 %copy-start.19 = (bf16[2048,256]{1,0:T(8,128)(2,1)S(1)}, bf16[2048,256]{1,0:T(8,128)(2,1)}, u32[]{:S(2)}) copy-start(bf16[2048,256]{1,0:T(8,128)(2,1)} %param.19) | copy-start | bytes 3145732
  62.9 0.9 copy-start
  62.9 0.9 copy-start.1
  62.9 0.9 copy-start.2
  63.8 14.0 %copy-start.17 = (bf16[1024,2048]{1,0:T(8,128)(2,1)S(1)}, bf16[1024,2048]{1,0:T(8,128)(2,1)}, u32[]{:S(2)}) copy-start(bf16[1024,2048]{1,0:T(8,128)(2,1)} %param.27) | copy-start | bytes 12582916
  80.1 54.9 %reduce-scatter.5.cloned.1.call-start = ((), (), s32[]{:S(2)}) async-start(), calls=%async_computation.3 | async-start | bytes 1310720 | tf_op jit(solution)/shard_map/reduce_scatter | solution.py:362
  80.3 1.5 copy-start.20
  90.2 14.0 %copy-start.18 = (bf16[1024,2048]{1,0:T(8,128)(2,1)S(1)}, bf16[1024,2048]{1,0:T(8,128)(2,1)}, u32[]{:S(2)}) copy-start(bf16[1024,2048]{1,0:T(8,128)(2,1)} %param.27) | copy-start | bytes 12582916
  104.2 2.6 %copy-start.10 = (s32[32]{0:T(128)S(1)}, s32[32]{0:T(128)}, u32[]{:S(2)}) copy-start(s32[32]{0:T(128)} %get-tuple-element.55.in_order) | copy-start | bytes 388
  106.8 28.3 %copy-start.7 = (bf16[256,512]{1,0:T(8,128)(2,1)S(1)}, bf16[256,512]{1,0:T(8,128)(2,1)}, u32[]{:S(2)}) copy-start(bf16[256,512]{1,0:T(8,128)(2,1)} %reduce-scatter.3.cloned.1.call-done) | copy-start | bytes 786436
Sparse Core Ops, SparseCore 0:
  80.2 26.4 reduce-scatter.2
  109.1 25.8 reduce-scatter.4
